TPU v7x, 768 devices: a whole 4x8x12 slice. The times are simulated.
768 devices in a mesh: dp: 96 (over y, x, z_lo), node: 8 (over z_hi, core).
Axes of the slice: x: 4, y: 8, z: 12 (z_hi: 4, z_lo: 3; z = z_hi * 3 + z_lo), core: 2. Of those that a mesh axis runs over, the one named last changes fastest.
Arguments:
- acts: bfloat16 [98304, 8192], P(('dp', 'node')), may hold values from -6 to 6
- cotangent: bfloat16 [98304, 512], P(('dp', 'node')), may hold values from -6 to 6
- w_values: bfloat16 [8192, 512], P('node'), may hold values from -0.25 to 0.25
- w_scales: float32 [64], P('node'), may hold values from 0.5 to 4
Outputs:
- input_grad: bfloat16 [98304, 8192], P('dp', 'node')
- weight_grad: float32 [8192, 512], P('node')
All inputs are finite; a program needn't handle non-finite values. Where the computation divides by a largest or mean magnitude, that divisor is 1e-20 or more.
Results may differ from a plain program's by a relative error of at most 0.012.
Values may be sent and summed in bfloat16 or wider, within the bound.
No kernel may reach another device: no remote copies, remote signals or barrier semaphores. Data moves between devices by JAX's collectives and lax.ppermute only.
A program may use at most 32 MiB of HBM per device.

v0:
```python
import jax
import jax.numpy as jnp
from jax import lax
from jax.sharding import PartitionSpec as P


def block_quant(grad):
    scale = jnp.max(jnp.abs(grad), axis=(-2, -1), keepdims=True) + 1e-06
    values = (grad / scale).astype(jnp.bfloat16)
    return (values, scale)


def input_gradient(peers, w_values, w_scales):
    head = w_values.shape[1]
    local_blocks = w_values.shape[0] // 128
    weight = (
        (w_values.astype(jnp.float32).reshape(local_blocks, 128, head) * w_scales[:, None, None])
        .reshape(local_blocks * 128, head)
        .astype(jnp.bfloat16)
    )
    columns = lax.dot_general(
        peers, weight, (((1,), (1,)), ((), ())), preferred_element_type=jnp.float32
    )
    return columns.astype(jnp.bfloat16)


def weight_gradient(columns, peers, tok_rows):
    nodes = lax.axis_size("node")
    owned = columns.shape[1]
    head = peers.shape[1]
    blocks = owned // 128
    stacked_x = columns.reshape(nodes, tok_rows, owned)
    stacked_y = peers.reshape(nodes, tok_rows, head)

    def add_source(total, pair):
        block_x, block_y = pair
        partial_value = lax.dot_general(
            block_x, block_y, (((0,), (0,)), ((), ())), preferred_element_type=jnp.float32
        )
        values, scale = block_quant(partial_value.reshape(blocks, 128, head))
        return (total + values.astype(jnp.float32) * scale, None)

    start = jnp.zeros((blocks, 128, head), jnp.float32)
    node_sum, unused = lax.scan(add_source, start, (stacked_x, stacked_y))
    rvalues, rscale = block_quant(node_sum)
    summed = lax.psum(rvalues.astype(jnp.float32) * rscale, "dp")
    factor = (tok_rows * nodes * lax.axis_size("dp")) ** (-0.5)
    return summed.reshape(owned, head) * factor


def local(acts, cotangent, w_values, w_scales):
    tok_rows = acts.shape[0]
    peers = lax.all_gather(cotangent, "node", axis=0, tiled=True)
    columns = lax.all_to_all(acts, "node", split_axis=1, concat_axis=0, tiled=True)
    input_grad = input_gradient(peers, w_values, w_scales)
    weight_grad = weight_gradient(columns, peers, tok_rows)
    return (input_grad, weight_grad)


def solution(mesh):
    placed = (P(("dp", "node"), None), P(("dp", "node"), None), P("node", None), P("node"))
    return jax.shard_map(
        local,
        mesh=mesh,
        in_specs=placed,
        out_specs=(P("dp", "node"), P("node", None)),
        check_vma=False,
    )
```

profile of v0, /device:TPU:192, one launch (start us, length us, event | category | flops | bytes accessed | tf_op | source)
XLA Modules:
  0.0 1260.6 jit_solution(201841965322007204)
XLA Ops:
  7.2 4.1 copy.6
  11.3 12.3 all-to-all-start
  24.4 49.5 %all-gather.2.cloned.1.call-done = bf16[1024,512]{1,0:T(8,128)(2,1)} async-done(((bf16[128,512]{1,0:T(8,128)(2,1)}), bf16[1024,512]{1,0:T(8,128)(2,1)}) %all-gather.2.cloned.1.call-update) | async-done | bytes 1048592 | tf_op jit(solution)/shard_map/all_gather | solution.py:53
  73.8 30.1 %all-to-all-done = bf16[128,8,1024]{0,2,1:T(8,128)(2,1)} async-done(((bf16[128,8,1024]{0,2,1:T(8,128)(2,1)}), bf16[128,8,1024]{0,2,1:T(8,128)(2,1)}, u32[]{:S(2)}, u32[]{:S(2)}) %all-to-all-start) | async-done | bytes 2097184 | tf_op jit(solution)/shard_map/all_to_all | solution.py:54
  103.9 45.7 %while.11 = (s32[]{:T(128)}, f32[8,128,512]{2,1,0:T(8,128)}, bf16[8,128,1024]{1,2,0:T(8,128)(2,1)}, bf16[8,128,512]{2,1,0:T(8,128)(2,1)}, s32[]{:T(128)}, /*index=5*/s32[]{:T(128)}) while((s32[]{:T(128)}, f32[8,128,512]{2,1,0:T(8,128)}, bf16[8,128,1024]{1,2,0:T(8,128)(2,1)}, bf16[8,128,512]{2,1,0:T(8,128)(2,1)}, s32[]{:T(128)}, ...), condition=%wide.region_2.3_spmd.clone, body=%wide.region_0.2_spmd.clone.sunk | while | flops 138412032 | bytes 9306835 | solution.py:44
  103.9 1.0 constant_dynamic-slice_fusion.2
  104.9 1.4 abs_reduce_fusion.3
  106.3 1.9 select_add_fusion.2
  108.2 1.0 constant_dynamic-slice_fusion.2
  109.2 1.4 abs_reduce_fusion.3
  110.7 3.5 select_add_fusion.2
  115.1 1.5 abs_reduce_fusion.3
  116.6 3.5 select_add_fusion.2
  121.0 1.4 abs_reduce_fusion.3
  122.5 3.5 select_add_fusion.2
  126.9 1.5 abs_reduce_fusion.3
  128.4 3.5 select_add_fusion.2
  132.9 1.5 abs_reduce_fusion.3
  134.3 3.5 select_add_fusion.2
  137.8 1.0 constant_dynamic-slice_fusion.2
  138.8 1.4 abs_reduce_fusion.3
  140.2 3.5 select_add_fusion.2
  143.7 1.0 constant_dynamic-slice_fusion.2
  144.7 1.5 abs_reduce_fusion.3
  146.2 3.5 select_add_fusion.2
  149.6 2.0 abs_reduce_fusion.1
  151.9 1.7 convert_multiply_fusion
  153.6 1.1 copy-done.2
  154.7 2.5 convert_bitcast_fusion
  157.3 2.6 copy.7
  159.8 1090.7 %all-reduce.2.cloned.1.call-done = f32[8,128,512]{2,1,0:T(8,128)} async-done(((f32[8,128,512]{2,1,0:T(8,128)}), f32[8,128,512]{2,1,0:T(8,128)}) %all-reduce.2.cloned.1.call-update) | async-done | bytes 2097168 | tf_op jit(solution)/shard_map/psum | solution.py:46
  1250.5 3.3 broadcast_multiply_fusion
  (24 shorter events, 5.0 us)
Async XLA Ops:
  7.2 146.4 %copy-start = (f32[8]{0:T(128)S(1)}, f32[8]{0:T(128)}, u32[]{:S(2)}) copy-start(f32[8]{0:T(128)} %param.9) | copy-start | bytes 100
  11.3 92.7 %all-to-all-start = ((bf16[128,8,1024]{0,2,1:T(8,128)(2,1)}), bf16[128,8,1024]{0,2,1:T(8,128)(2,1)}, u32[]{:S(2)}, u32[]{:S(2)}) async-start(bf16[128,8,1024]{0,2,1:T(8,128)(2,1)} %bitcast.2), calls=%async_computation | async-start | bytes 4194304 | tf_op jit(solution)/shard_map/all_to_all | solution.py:54
  23.6 50.2 %all-gather.2.cloned.1.call-start = ((), (), s32[]{:S(2)}) async-start(), calls=%async_computation.1 | async-start | bytes 1179648 | tf_op jit(solution)/shard_map/all_gather | solution.py:53
  24.3 1226.2 %all-reduce.2.cloned.1.call-start = ((), (), s32[]{:S(2)}) async-start(), calls=%async_computation.2 | async-start | bytes 4194304 | tf_op jit(solution)/shard_map/psum | solution.py:46
  149.6 2.2 copy-start.1
  153.5 1.2 copy-start.2
Sparse Core Ops, SparseCore 0:
  26.9 46.9 all-gather.1
  153.7 1096.8 all-reduce.1
where the time goes:
time: 1260 us
  waiting for transfers between devices  1170 us (93%)
  other arithmetic  33.3 us (3%)
  local copies, waits for them, and re-layouts  15.8 us (1%)
  matrix products  14.1 us (1%)
  between operations  14.1 us (1%)
    psum x1, waiting for transfers between devices, weight_gradient(): summed = lax.psum(rvalues.astype(jnp.float32) * rscale, 'dp')  1090 us
    all_gather x1, waiting for transfers between devices, local(): peers = lax.all_gather(cotangent, 'node', axis=0, tiled=True)  49.5 us
    all_to_all x1, waiting for transfers between devices, local(): lax.all_to_all(acts, 'node', split_axis=1, concat_axis=0, tiled=True)  30.1 us
    add x8, other arithmetic, add_source(): return (total + values.astype(jnp.float32) * scale, None)  26.3 us
  transfers between devices with their start and end apart: 3, of which 3 were waited for; matrix products, arithmetic and copies ran while one was open for 0% of the time, Pallas kernels for 0%

commit v1 on v0

v1 whole, which is shorter than its diff:
```python
import jax
import jax.numpy as jnp
from jax import lax
from jax.sharding import Mesh
from jax.sharding import PartitionSpec as P

AXES = ("y", "x", "zl", "zh", "c")
SIZES = (8, 4, 3, 4, 2)


def input_gradient(peers, w_values, w_scales):
    head = w_values.shape[1]
    blocks = w_values.shape[0] // 128
    weight = (
        (w_values.astype(jnp.float32).reshape(blocks, 128, head) * w_scales[:, None, None])
        .reshape(blocks * 128, head)
        .astype(jnp.bfloat16)
    )
    columns = lax.dot_general(
        peers, weight, (((1,), (1,)), ((), ())), preferred_element_type=jnp.float32
    )
    return columns.astype(jnp.bfloat16)


def exchange(value, axes):
    return lax.all_to_all(value, axes, split_axis=0, concat_axis=0, tiled=True)


def spread(value, axes, size):
    copies = lax.optimization_barrier(jnp.broadcast_to(value[None], (size,) + value.shape))
    return exchange(copies, axes)


def weight_gradient(acts, cotangent, factor):
    tok, width = acts.shape
    head = cotangent.shape[1]
    ny, nx, nzl, nzh, nc = SIZES
    owned = width // (nzh * nc)
    part = owned // nx
    rows = part // ny
    by_x = jnp.moveaxis(acts.reshape(tok, nzh * nc, nx, part), 2, 0).reshape(nx, tok, nzh * nc * part)
    both = jnp.concatenate([by_x, jnp.broadcast_to(cotangent[None], (nx, tok, head))], axis=2)
    got = exchange(both, "x").reshape(nx * tok, nzh * nc * part + head)
    partial = lax.dot_general(
        got[:, : nzh * nc * part],
        got[:, nzh * nc * part :],
        (((0,), (0,)), ((), ())),
        preferred_element_type=jnp.float32,
    )
    partial = partial.reshape(nzh, nc, ny, rows, head).transpose(1, 2, 0, 3, 4)
    over_c = exchange(partial.astype(jnp.bfloat16), "c")
    chip = jnp.sum(over_c.astype(jnp.float32), axis=0).astype(jnp.bfloat16)
    over_y = jnp.sum(exchange(chip, "y").astype(jnp.float32), axis=0).astype(jnp.bfloat16)
    half = rows // 2
    slots = over_y.reshape(nzh, 2, half, head)
    slots = jnp.concatenate([slots, jnp.zeros((nzh, 1, half, head), jnp.bfloat16)], axis=1)
    slots = slots.reshape(nzh * nzl, half, head)
    total = jnp.sum(exchange(slots, ("zh", "zl")).astype(jnp.float32), axis=0).astype(jnp.bfloat16)
    back = spread(total, ("y", "zl"), ny * nzl).reshape(ny, nzl, half, head)
    back = back[:, :2].reshape(part, head)
    full = spread(back, "x", nx).reshape(owned, head)
    return full.astype(jnp.float32) * factor


def local(acts, cotangent, w_values, w_scales):
    tokens = acts.shape[0] * 768
    peers = lax.all_gather(cotangent, ("zh", "c"), axis=0, tiled=True)
    input_grad = input_gradient(peers, w_values, w_scales)
    weight_grad = weight_gradient(acts, cotangent, tokens ** (-0.5))
    return (input_grad, weight_grad)


def solution(mesh):
    fine = Mesh(mesh.devices.reshape(SIZES), AXES)
    dp, node = ("y", "x", "zl"), ("zh", "c")
    placed = (P(dp + node, None), P(dp + node, None), P(node, None), P(node))
    return jax.shard_map(
        local,
        mesh=fine,
        in_specs=placed,
        out_specs=(P(dp, node), P(node, None)),
        check_vma=False,
    )
```

time: 1260 us -> 176 us (0.14)
  the two profiles are of different devices: /device:TPU:192 before, /device:TPU:2 now
where the time goes in v1:
time: 176 us; the launch traced here: 175 us
  blocking collectives  99.2 us (56%)
  starting transfers between devices  22.2 us (13%)
  waiting for transfers between devices  18.2 us (10%)
  between operations  14.1 us (8%)
  local copies, waits for them, and re-layouts  13.4 us (8%)
  matrix products  5.8 us (3%)
  other arithmetic  2.63 us (1%)
    all_to_all x4, blocking collectives, exchange(): return lax.all_to_all(value, axes, split_axis=0, concat_axis=0, tiled=True)  99.2 us
    all_to_all x2, starting transfers between devices, exchange(): return lax.all_to_all(value, axes, split_axis=0, concat_axis=0, tiled=True)  22.1 us
    all_to_all x2, waiting for transfers between devices, exchange(): return lax.all_to_all(value, axes, split_axis=0, concat_axis=0, tiled=True)  17.5 us
    unnamed x7, local copies, waits for them, and re-layouts  6.76 us
  transfers between devices with their start and end apart: 3, of which 2 were waited for; matrix products, arithmetic and copies ran while one was open for 4% of the time, Pallas kernels for 0%

profile of v1, /device:TPU:2, one launch (start us, length us, event | category | flops | bytes accessed | tf_op | source)
XLA Modules:
  0.0 175.4 jit_solution(14855794907877140191)
XLA Ops:
  7.2 0.0 copy-start
  7.2 4.1 %copy.29 = bf16[128,8192]{0,1:T(8,128)(2,1)} copy(bf16[128,8192]{1,0:T(8,128)(2,1)} %param.4) | data formatting | bytes 4194304 | tf_op args[0]
  11.3 0.0 copy-start.1
  11.3 1.8 %copy.30 = bf16[4,128,8,256]{1,3,2,0:T(8,128)(2,1)S(1)} copy(bf16[4,128,8,256]{1,3,0,2:T(8,128)(2,1)} %bitcast.21) | data formatting | bytes 4194304 | tf_op jit(solution)/shard_map/transpose | solution.py:41
  13.0 0.0 copy-done.1
  13.0 0.1 copy.31
  13.2 0.1 broadcast_in_dim.8
  13.2 0.2 pad_maximum_fusion
  13.4 35.1 %all_to_all.30 = bf16[4,128,2560]{1,2,0:T(8,128)(2,1)S(1)} all-to-all(bf16[4,128,2560]{1,2,0:T(8,128)(2,1)S(1)} %pad_maximum_fusion), channel_id=1, replica_groups=mesh['y'=8,'x'=4,'zl'=3,'zh'=4,'c'=2] {'x'}, dimensions={0} | all-to-all | bytes 5242880 | tf_op jit(solution)/shard_map/all_to_all | solution.py:26
  48.5 2.6 %copy.32 = bf16[4,128,2560]{2,1,0:T(8,128)(2,1)} copy(bf16[4,128,2560]{1,2,0:T(8,128)(2,1)S(1)} %all_to_all.30) | data formatting | bytes 5242880 | tf_op jit(solution)/shard_map/all_to_all | solution.py:26
  51.1 3.0 %convolution_convert_fusion = bf16[2048,512]{1,0:T(8,128)(2,1)S(1)} fusion(bf16[512,2560]{1,0:T(8,128)(2,1)} %bitcast.22), kind=kOutput, calls=%fused_computation | convolution fusion | flops 1074790400 | bytes 4718592 | tf_op jit(solution)/shard_map/dot_general | solution.py:44
  54.1 0.2 copy.39
  54.3 5.4 %all_to_all.31 = bf16[2,8,4,32,512]{4,3,1,2,0:T(8,128)(2,1)S(1)} all-to-all(bf16[2,8,4,32,512]{4,3,1,2,0:T(8,128)(2,1)S(1)} %bitcast.20), channel_id=1, replica_groups=mesh['y'=8,'x'=4,'zl'=3,'zh'=4,'c'=2] {'c'}, dimensions={0} | all-to-all | bytes 4194304 | tf_op jit(solution)/shard_map/all_to_all | solution.py:26
  59.7 0.6 reduce_sum.36
  60.4 0.1 copy.35
  60.5 35.9 %all_to_all.32 = bf16[8,4,32,512]{3,2,1,0:T(8,128)(2,1)S(1)} all-to-all(bf16[8,4,32,512]{3,2,1,0:T(8,128)(2,1)S(1)} %copy.35), channel_id=1, replica_groups=mesh['y'=8,'x'=4,'zl'=3,'zh'=4,'c'=2] {'y'}, dimensions={0} | all-to-all | bytes 2097152 | tf_op jit(solution)/shard_map/all_to_all | solution.py:26
  96.4 0.2 reduce_sum.37
  96.6 0.7 concatenate.7
  97.3 15.2 %all-to-all-start.3 = ((bf16[12,16,512]{2,1,0:T(8,128)(2,1)}), bf16[12,16,512]{2,1,0:T(8,128)(2,1)S(1)}, u32[]{:S(2)}, u32[]{:S(2)}) async-start(bf16[12,16,512]{2,1,0:T(8,128)(2,1)} %bitcast.9), calls=%async_computation.3 | async-start | bytes 393216 | tf_op jit(solution)/shard_map/all_to_all | solution.py:26
  112.4 0.0 all-gather.2.cloned.1.call-start
  112.5 0.7 all-gather.2.cloned.1.call-update
  113.2 12.2 %all-to-all-done.3 = bf16[12,16,512]{2,1,0:T(8,128)(2,1)S(1)} async-done(((bf16[12,16,512]{2,1,0:T(8,128)(2,1)}), bf16[12,16,512]{2,1,0:T(8,128)(2,1)S(1)}, u32[]{:S(2)}, u32[]{:S(2)}) %all-to-all-start.3) | async-done | bytes 196640 | tf_op jit(solution)/shard_map/all_to_all | solution.py:26
  125.4 22.7 %all_to_all.33 = bf16[24,16,512]{2,1,0:T(8,128)(2,1)S(1)} all-to-all(bf16[24,16,512]{2,1,0:T(8,128)(2,1)S(1)} %broadcast_in_dim.9), channel_id=1, replica_groups=mesh['y'=8,'x'=4,'zl'=3,'zh'=4,'c'=2] {'y','zl'}, dimensions={0} | all-to-all | bytes 786432 | tf_op jit(solution)/shard_map/all_to_all | solution.py:26
  148.2 1.1 broadcast_in_dim.11
  149.2 7.0 %all-to-all-start.5 = ((bf16[4,256,512]{2,1,0:T(8,128)(2,1)}), bf16[4,256,512]{2,1,0:T(8,128)(2,1)S(1)}, u32[]{:S(2)}, u32[]{:S(2)}) async-start(bf16[4,256,512]{2,1,0:T(8,128)(2,1)} %broadcast_in_dim.11), calls=%async_computation.5 | async-start | bytes 2097152 | tf_op jit(solution)/shard_map/all_to_all | solution.py:26
  156.2 0.0 copy-done
  156.2 0.1 broadcast_bitcast_fusion
  156.3 0.0 all-gather.2.cloned.1.call-done
  156.3 2.8 %convert_bitcast_fusion = bf16[1024,1024]{0,1:T(8,128)(2,1)S(1)} fusion(bf16[1024,512]{1,0:T(8,128)(2,1)} %all-gather.2.cloned.1.call-done, bf16[1024,512]{1,0:T(8,128)(2,1)} %param.6, f32[1024]{0:T(1024)S(1)} %broadcast_bitcast_fusion), kind=kOutput, calls=%fused_computation.5 | convolution fusion | flops 1076363264 | bytes 4198400 | tf_op jit(solution)/shard_map/dot_general | solution.py:19
  159.1 2.6 %copy.36 = bf16[1024,1024]{1,0:T(8,128)(2,1)} copy(bf16[1024,1024]{0,1:T(8,128)(2,1)S(1)} %convert_bitcast_fusion) | data formatting | bytes 4194304
  161.7 5.3 %all-to-all-done.5 = bf16[4,256,512]{2,1,0:T(8,128)(2,1)S(1)} async-done(((bf16[4,256,512]{2,1,0:T(8,128)(2,1)}), bf16[4,256,512]{2,1,0:T(8,128)(2,1)S(1)}, u32[]{:S(2)}, u32[]{:S(2)}) %all-to-all-start.5) | async-done | bytes 1048608 | tf_op jit(solution)/shard_map/all_to_all | solution.py:26
  167.0 1.6 convert_multiply_fusion
  (3 shorter events, 0.1 us)
Async XLA Ops:
  7.2 149.0 %copy-start = (f32[8]{0:T(128)S(1)}, f32[8]{0:T(128)}, u32[]{:S(2)}) copy-start(f32[8]{0:T(128)} %param.7) | copy-start | bytes 100
  11.3 1.8 %copy-start.1 = (bf16[128,512]{1,0:T(8,128)(2,1)S(1)}, bf16[128,512]{1,0:T(8,128)(2,1)}, u32[]{:S(2)}) copy-start(bf16[128,512]{1,0:T(8,128)(2,1)} %param.5) | copy-start | bytes 393220
  97.3 28.1 %all-to-all-start.3 = ((bf16[12,16,512]{2,1,0:T(8,128)(2,1)}), bf16[12,16,512]{2,1,0:T(8,128)(2,1)S(1)}, u32[]{:S(2)}, u32[]{:S(2)}) async-start(bf16[12,16,512]{2,1,0:T(8,128)(2,1)} %bitcast.9), calls=%async_computation.3 | async-start | bytes 393216 | tf_op jit(solution)/shard_map/all_to_all | solution.py:26
  112.4 43.8 %all-gather.2.cloned.1.call-start = ((), (), s32[]{:S(2)}) async-start(), calls=%async_computation.6 | async-start | bytes 1179648 | tf_op jit(solution)/shard_map/all_gather | solution.py:67
  149.2 17.7 %all-to-all-start.5 = ((bf16[4,256,512]{2,1,0:T(8,128)(2,1)}), bf16[4,256,512]{2,1,0:T(8,128)(2,1)S(1)}, u32[]{:S(2)}, u32[]{:S(2)}) async-start(bf16[4,256,512]{2,1,0:T(8,128)(2,1)} %broadcast_in_dim.11), calls=%async_computation.5 | async-start | bytes 2097152 | tf_op jit(solution)/shard_map/all_to_all | solution.py:26
Sparse Core Ops, SparseCore 0:
  115.7 35.3 all-gather.1

commit v2 on v1

v2 whole, which is shorter than its diff:
```python
import jax
import jax.numpy as jnp
from jax import lax
from jax.experimental import pallas as pl
from jax.experimental.pallas import tpu as pltpu
from jax.sharding import Mesh
from jax.sharding import PartitionSpec as P

AXES = ("y", "x", "zl", "zh", "c")
NY, NX, NZL, NZH, NC = SIZES = (8, 4, 3, 4, 2)
NODE = NZH * NC
SMALL = pltpu.CompilerParams(vmem_limit_bytes=12 * 2**20)


def exchange(value, axes):
    return lax.all_to_all(value, axes, split_axis=0, concat_axis=0, tiled=True)


def spread(value, axes, size):
    copies = lax.optimization_barrier(jnp.broadcast_to(value[None], (size,) + value.shape))
    return exchange(copies, axes)


def lay_out(acts, cotangent):
    tok, width = acts.shape
    head = cotangent.shape[1]
    part = width // (NODE * NX)
    step = 32

    def kernel(acts_ref, cot_ref, out_ref):
        for x in range(NX):
            for n in range(NODE):
                out_ref[x, :, n * part : (n + 1) * part] = acts_ref[:, pl.ds((n * NX + x) * part, part)]
            out_ref[x, :, NODE * part :] = cot_ref[...]

    return pl.pallas_call(
        kernel,
        grid=(tok // step,),
        in_specs=[
            pl.BlockSpec((step, width), lambda i: (i, 0)),
            pl.BlockSpec((step, head), lambda i: (i, 0)),
        ],
        out_specs=pl.BlockSpec((NX, step, NODE * part + head), lambda i: (0, i, 0)),
        out_shape=jax.ShapeDtypeStruct((NX, tok, NODE * part + head), jnp.bfloat16),
        compiler_params=SMALL,
        cost_estimate=pl.CostEstimate(flops=0, bytes_accessed=2 * NX * tok * (NODE * part + head) * 2, transcendentals=0),
    )(acts, cotangent)


def product(got, head, after):
    tokens, width = got.shape
    part = (width - head) // NODE
    rows = part // NY

    def kernel(acts_ref, cot_ref, *refs):
        out_ref = refs[-1]
        value = lax.dot_general(
            acts_ref[...], cot_ref[...], (((0,), (0,)), ((), ())), preferred_element_type=jnp.float32
        )
        out_ref[0, :, 0] = value.astype(jnp.bfloat16).reshape(NY, rows, head)

    return pl.pallas_call(
        kernel,
        grid=(NODE,),
        in_specs=[
            pl.BlockSpec((tokens, part), lambda n: (0, n)),
            pl.BlockSpec((tokens, head), lambda n: (0, NODE * part // head)),
        ]
        + [pl.BlockSpec(memory_space=pl.ANY)] * len(after),
        out_specs=pl.BlockSpec((1, NY, 1, rows, head), lambda n: (n % NC, 0, n // NC, 0, 0)),
        out_shape=jax.ShapeDtypeStruct((NC, NY, NZH, rows, head), jnp.bfloat16),
        compiler_params=SMALL,
        cost_estimate=pl.CostEstimate(
            flops=2 * tokens * NODE * part * head,
            bytes_accessed=(tokens * width + NODE * part * head) * 2,
            transcendentals=0,
        ),
    )(got, got, *after)


def add(value):
    return jnp.sum(value.astype(jnp.float32), axis=0).astype(jnp.bfloat16)


def add_copies(value, copies, axis, after=()):
    shape = value.shape[1:]
    out = shape[:axis] + (copies,) + shape[axis:]

    def kernel(value_ref, *refs):
        total = value_ref[0].astype(jnp.float32)
        for i in range(1, value.shape[0]):
            total = total + value_ref[i].astype(jnp.float32)
        total = total.astype(jnp.bfloat16)
        for i in range(copies):
            refs[-1][(slice(None),) * axis + (i,)] = total

    return pl.pallas_call(
        kernel,
        in_specs=[pl.BlockSpec(memory_space=pltpu.VMEM)] + [pl.BlockSpec(memory_space=pl.ANY)] * len(after),
        out_specs=pl.BlockSpec(memory_space=pltpu.VMEM),
        out_shape=jax.ShapeDtypeStruct(out, jnp.bfloat16),
        compiler_params=SMALL,
        cost_estimate=pl.CostEstimate(flops=value.size, bytes_accessed=value.size * 2, transcendentals=0),
    )(value, *after)


def input_gradient(peers, w_values, w_scales):
    head = w_values.shape[1]
    blocks = w_values.shape[0] // 128
    weight = (
        (w_values.astype(jnp.float32).reshape(blocks, 128, head) * w_scales[:, None, None])
        .reshape(blocks * 128, head)
        .astype(jnp.bfloat16)
    )
    columns = lax.dot_general(
        peers, weight, (((1,), (1,)), ((), ())), preferred_element_type=jnp.float32
    )
    return columns.astype(jnp.bfloat16)


def gather_zh(cotangent):
    return [cotangent] + [
        lax.ppermute(cotangent, "zh", [(i, (i + k) % NZH) for i in range(NZH)]) for k in range(1, NZH)
    ]


def gather_node(mine):
    here = lax.axis_index("zh")
    stack = jnp.stack(mine)
    ordered = jnp.concatenate(
        [lax.dynamic_slice_in_dim(stack, (here - j) % NZH, 1, 0) for j in range(NZH)], axis=0
    )
    other = lax.ppermute(ordered, "c", [(0, 1), (1, 0)])
    first = lax.axis_index("c") == 0
    return jnp.stack([jnp.where(first, ordered, other), jnp.where(first, other, ordered)], axis=1)


def local(acts, cotangent, w_values, w_scales):
    tok, width = acts.shape
    head = cotangent.shape[1]
    owned = width // NODE
    part = owned // NX
    rows = part // NY
    factor = (tok * NY * NX * NZL * NZH * NC) ** (-0.5)

    got = exchange(lay_out(acts, cotangent), "x")
    mine = gather_zh(cotangent)
    partial = product(got.reshape(NX * tok, NODE * part + head), head, mine[1:])
    chip = add(exchange(partial, "c"))

    over_y = exchange(chip, "y")
    peers = gather_node(mine).reshape(NODE * tok, head)
    input_grad = input_gradient(peers, w_values, w_scales)

    slots = add_copies(over_y, NZL, 1, [input_grad]).reshape(NZH * NZL, rows, head)
    total = add_copies(exchange(slots, ("zh", "zl")), NY, 0)
    back = exchange(total, "y").reshape(part, head)
    full = spread(back, "x", NX).reshape(owned, head)
    return (input_grad, full.astype(jnp.float32) * factor)


def solution(mesh):
    fine = Mesh(mesh.devices.reshape(SIZES), AXES)
    dp, node = ("y", "x", "zl"), ("zh", "c")
    placed = (P(dp + node, None), P(dp + node, None), P(node, None), P(node))
    return jax.shard_map(
        local,
        mesh=fine,
        in_specs=placed,
        out_specs=(P(dp, node), P(node, None)),
        check_vma=False,
    )
```

time: 176 us -> 156 us (0.89)
  the two profiles are of different devices: /device:TPU:2 before, /device:TPU:64 now
where the time goes in v2:
time: 156 us
  blocking collectives  69.9 us (45%)
  starting transfers between devices  36.5 us (23%)
  waiting for transfers between devices  34.4 us (22%)
  local copies, waits for them, and re-layouts  5.31 us (3%)
  Pallas kernels  3.81 us (2%)
  other arithmetic  3.67 us (2%)
    all_to_all x4, blocking collectives, exchange(): return lax.all_to_all(value, axes, split_axis=0, concat_axis=0, tiled=True)  69.9 us
    ppermute x3, starting transfers between devices, gather_zh(): lax.ppermute(cotangent, 'zh', [(i, (i + k) % NZH) for i in range(NZH)])  23.1 us
    all_to_all x2, waiting for transfers between devices, exchange(): return lax.all_to_all(value, axes, split_axis=0, concat_axis=0, tiled=True)  22.3 us
    all_to_all x2, starting transfers between devices, exchange(): return lax.all_to_all(value, axes, split_axis=0, concat_axis=0, tiled=True)  11.5 us
    ppermute x3, waiting for transfers between devices, gather_zh(): lax.ppermute(cotangent, 'zh', [(i, (i + k) % NZH) for i in range(NZH)])  10.3 us
    unnamed x14, local copies, waits for them, and re-layouts  5.01 us
    pallas_call x1, Pallas kernels, product(): pl.pallas_call(kernel, grid=(NODE,), in_specs=[pl.BlockSpec((tokens, part...  3.22 us
  transfers between devices with their start and end apart: 6, of which 4 were waited for; matrix products, arithmetic and copies ran while one was open for 1% of the time, Pallas kernels for 0%

profile of v2, /device:TPU:64, one launch (start us, length us, event | category | flops | bytes accessed | tf_op | source)
XLA Modules:
  0.0 155.9 jit_solution(7351434095467204254)
XLA Ops:
  0.7 1.6 %copy-done.2 = bf16[128,8192]{1,0:T(8,128)(2,1)S(1)} copy-done((bf16[128,8192]{1,0:T(8,128)(2,1)S(1)}, bf16[128,8192]{1,0:T(8,128)(2,1)}, u32[]{:S(2)}) %copy-start.2) | copy-done | bytes 2097176
  2.2 0.9 copy-done.4
  3.1 0.4 shard_map.59
  3.6 1.5 copy-done.1
  5.1 4.4 %all-to-all-start = ((bf16[4,128,2560]{2,1,0:T(8,128)(2,1)}), bf16[4,128,2560]{2,1,0:T(8,128)(2,1)S(1)}, u32[]{:S(2)}, u32[]{:S(2)}) async-start(bf16[4,128,2560]{2,1,0:T(8,128)(2,1)} %copy-done.1), calls=%async_computation | async-start | bytes 5242880 | tf_op jit(solution)/shard_map/all_to_all | solution.py:16
  9.5 14.2 %collective-permute-start.1 = (bf16[128,512]{1,0:T(8,128)(2,1)S(1)}, bf16[128,512]{1,0:T(8,128)(2,1)S(1)}, u32[]{:S(2)}, u32[]{:S(2)}) collective-permute-start(bf16[128,512]{1,0:T(8,128)(2,1)S(1)} %copy-done.5), channel_id=1, source_target_pairs={{0,4},{2,6},{4,0},{6,2},{1,5},{3,7},{5,1},{7,3},{8,12},{10,14},{12... | collective-permute-start | bytes 393224 | tf_op jit(solution)/shard_map/ppermute | solution.py:123
  23.7 5.8 %collective-permute-start = (bf16[128,512]{1,0:T(8,128)(2,1)S(1)}, bf16[128,512]{1,0:T(8,128)(2,1)S(1)}, u32[]{:S(2)}, u32[]{:S(2)}) collective-permute-start(bf16[128,512]{1,0:T(8,128)(2,1)S(1)} %copy-done.5), channel_id=1, source_target_pairs={{0,2},{2,4},{4,6},{6,0},{1,3},{3,5},{5,7},{7,1},{8,10},{10,12},{12... | collective-permute-start | bytes 393224 | tf_op jit(solution)/shard_map/ppermute | solution.py:123
  29.5 3.0 %collective-permute-start.2 = (bf16[128,512]{1,0:T(8,128)(2,1)S(1)}, bf16[128,512]{1,0:T(8,128)(2,1)S(1)}, u32[]{:S(2)}, u32[]{:S(2)}) collective-permute-start(bf16[128,512]{1,0:T(8,128)(2,1)S(1)} %copy-done.5), channel_id=1, source_target_pairs={{0,6},{2,0},{4,2},{6,4},{1,7},{3,1},{5,3},{7,5},{8,14},{10,8},{12,... | collective-permute-start | bytes 393224 | tf_op jit(solution)/shard_map/ppermute | solution.py:123
  32.6 7.8 %collective-permute-done.refs_0_ = bf16[128,512]{1,0:T(8,128)(2,1)S(1)} collective-permute-done((bf16[128,512]{1,0:T(8,128)(2,1)S(1)}, bf16[128,512]{1,0:T(8,128)(2,1)S(1)}, u32[]{:S(2)}, u32[]{:S(2)}) %collective-permute-start) | collective-permute-done | bytes 131104 | tf_op jit(solution)/shard_map/ppermute | solution.py:123
  40.5 2.4 %collective-permute-done.2.refs_2_ = bf16[128,512]{1,0:T(8,128)(2,1)S(1)} collective-permute-done((bf16[128,512]{1,0:T(8,128)(2,1)S(1)}, bf16[128,512]{1,0:T(8,128)(2,1)S(1)}, u32[]{:S(2)}, u32[]{:S(2)}) %collective-permute-start.2) | collective-permute-done | bytes 131104 | tf_op jit(solution)/shard_map/ppermute | solution.py:123
  42.9 3.2 %shard_map.60 = bf16[2,8,4,32,512]{4,3,2,1,0:T(8,128)(2,1)S(1)} custom-call(bf16[512,2560]{1,0:T(8,128)(2,1)S(1)} %bitcast.16, bf16[512,2560]{1,0:T(8,128)(2,1)S(1)} %bitcast.17, bf16[128,512]{1,0:T(8,128)(2,1)S(1)} %collective-permute-done.refs_0_, bf16[128,512]{1,0:T(8,128)(2,1)S(1)} %collective-permute-done.1.refs_1_, ...), custom_call_target="tpu_custom_call" | custom-call | flops 1073741824 | bytes 4718592 | tf_op jit(solution)/shard_map/pallas_call | solution.py:62
  46.1 5.4 %all_to_all.30 = bf16[2,8,4,32,512]{4,3,2,1,0:T(8,128)(2,1)S(1)} all-to-all(bf16[2,8,4,32,512]{4,3,2,1,0:T(8,128)(2,1)S(1)} %shard_map.60), channel_id=1, replica_groups=mesh['y'=8,'x'=4,'zl'=3,'zh'=4,'c'=2] {'c'}, dimensions={0} | all-to-all | bytes 4194304 | tf_op jit(solution)/shard_map/all_to_all | solution.py:16
  51.6 1.7 %reduce_sum.12 = bf16[8,4,32,512]{3,2,1,0:T(8,128)(2,1)} reduce(bf16[2,8,4,32,512]{4,3,2,1,0:T(8,128)(2,1)S(1)} %all_to_all.30, bf16[]{:T(256)} %constant.46.clone.1), dimensions={0}, to_apply=%region_0.0 | reduce | flops 524288 | bytes 3145730 | tf_op jit(solution)/shard_map/reduce_sum | solution.py:82
  53.3 7.1 %all-to-all-start.2 = ((bf16[8,4,32,512]{3,2,1,0:T(8,128)(2,1)}), bf16[8,4,32,512]{3,2,1,0:T(8,128)(2,1)S(1)}, u32[]{:S(2)}, u32[]{:S(2)}) async-start(bf16[8,4,32,512]{3,2,1,0:T(8,128)(2,1)} %reduce_sum.12), calls=%async_computation.2 | async-start | bytes 2097152 | tf_op jit(solution)/shard_map/all_to_all | solution.py:16
  60.4 0.1 pad_maximum_fusion.1
  60.5 0.1 pad_maximum_fusion.2
  60.6 1.9 %collective-permute-start.3 = (bf16[4,128,512]{2,1,0:T(8,128)(2,1)S(1)}, bf16[4,128,512]{2,1,0:T(8,128)(2,1)S(1)}, u32[]{:S(2)}, u32[]{:S(2)}) collective-permute-start(bf16[4,128,512]{2,1,0:T(8,128)(2,1)S(1)} %pad_maximum_fusion.2), channel_id=1, source_target_pairs={{0,1},{1,0},{2,3},{3,2},{4,5},{5,4},{6,7},{7,6},{8,9},{9,8},{10,11... | collective-permute-start | bytes 1572872 | tf_op jit(solution)/shard_map/ppermute | solution.py:133
  62.5 0.1 broadcast_bitcast_fusion
  62.6 1.8 %collective-permute-done.3 = bf16[4,128,512]{2,1,0:T(8,128)(2,1)S(1)} collective-permute-done((bf16[4,128,512]{2,1,0:T(8,128)(2,1)S(1)}, bf16[4,128,512]{2,1,0:T(8,128)(2,1)S(1)}, u32[]{:S(2)}, u32[]{:S(2)}) %collective-permute-start.3) | collective-permute-done | bytes 524320 | tf_op jit(solution)/shard_map/ppermute | solution.py:133
  64.4 0.1 select_bitcast_fusion.1
  64.5 0.1 pad_maximum_fusion
  64.6 0.1 copy.6
  64.7 1.0 copy-done.6
  65.7 1.4 convolution_convert_fusion.refs_0_
  67.1 22.3 %all-to-all-done.2.value_ref = bf16[8,4,32,512]{3,2,1,0:T(8,128)(2,1)S(1)} async-done(((bf16[8,4,32,512]{3,2,1,0:T(8,128)(2,1)}), bf16[8,4,32,512]{3,2,1,0:T(8,128)(2,1)S(1)}, u32[]{:S(2)}, u32[]{:S(2)}) %all-to-all-start.2) | async-done | bytes 1048608 | tf_op jit(solution)/shard_map/all_to_all | solution.py:16
  89.4 0.1 shard_map.61
  89.6 33.1 %all_to_all.31.value_ref = bf16[12,32,512]{2,1,0:T(8,128)(2,1)S(1)} all-to-all(bf16[12,32,512]{2,1,0:T(8,128)(2,1)S(1)} %bitcast.18), channel_id=1, replica_groups=mesh['y'=8,'x'=4,'zl'=3,'zh'=4,'c'=2] {'zh','zl'}, dimensions={0} | all-to-all | bytes 786432 | tf_op jit(solution)/shard_map/all_to_all | solution.py:16
  122.7 0.1 shard_map.62
  122.8 14.6 %all_to_all.32 = bf16[8,32,512]{2,1,0:T(8,128)(2,1)S(1)} all-to-all(bf16[8,32,512]{2,1,0:T(8,128)(2,1)S(1)} %shard_map.62), channel_id=1, replica_groups=mesh['y'=8,'x'=4,'zl'=3,'zh'=4,'c'=2] {'y'}, dimensions={0} | all-to-all | bytes 524288 | tf_op jit(solution)/shard_map/all_to_all | solution.py:16
  137.4 0.1 broadcast_in_dim.9
  137.4 16.8 %all_to_all.33 = bf16[4,256,512]{2,1,0:T(8,128)(2,1)S(1)} all-to-all(bf16[4,256,512]{2,1,0:T(8,128)(2,1)S(1)} %broadcast_in_dim.9), channel_id=1, replica_groups=mesh['y'=8,'x'=4,'zl'=3,'zh'=4,'c'=2] {'x'}, dimensions={0} | all-to-all | bytes 2097152 | tf_op jit(solution)/shard_map/all_to_all | solution.py:16
  154.2 1.6 %convert_multiply_fusion = f32[4,256,512]{2,1,0:T(8,128)} fusion(bf16[4,256,512]{2,1,0:T(8,128)(2,1)S(1)} %all_to_all.33), kind=kLoop, calls=%fused_computation | loop fusion | flops 1048576 | bytes 3145728 | tf_op jit(solution)/shard_map/mul | solution.py:159
  (13 shorter events, 0.1 us)
Async XLA Ops:
  0.6 61.9 %copy-start = (f32[8]{0:T(128)S(1)}, f32[8]{0:T(128)}, u32[]{:S(2)}) copy-start(f32[8]{0:T(128)} %param.7) | copy-start | bytes 100
  0.6 1.6 %copy-start.2 = (bf16[128,8192]{1,0:T(8,128)(2,1)S(1)}, bf16[128,8192]{1,0:T(8,128)(2,1)}, u32[]{:S(2)}) copy-start(bf16[128,8192]{1,0:T(8,128)(2,1)} %acts_ref.1) | copy-start | bytes 6291460
  2.2 0.9 copy-start.4
  3.6 1.5 copy-start.1
  5.1 4.4 %copy-start.5 = (bf16[128,512]{1,0:T(8,128)(2,1)S(1)}, bf16[128,512]{1,0:T(8,128)(2,1)}, u32[]{:S(2)}) copy-start(bf16[128,512]{1,0:T(8,128)(2,1)} %cot_ref.1) | copy-start | bytes 393220
  5.1 37.9 %all-to-all-start = ((bf16[4,128,2560]{2,1,0:T(8,128)(2,1)}), bf16[4,128,2560]{2,1,0:T(8,128)(2,1)S(1)}, u32[]{:S(2)}, u32[]{:S(2)}) async-start(bf16[4,128,2560]{2,1,0:T(8,128)(2,1)} %copy-done.1), calls=%async_computation | async-start | bytes 5242880 | tf_op jit(solution)/shard_map/all_to_all | solution.py:16
  9.5 23.1 %collective-permute-start.1 = (bf16[128,512]{1,0:T(8,128)(2,1)S(1)}, bf16[128,512]{1,0:T(8,128)(2,1)S(1)}, u32[]{:S(2)}, u32[]{:S(2)}) collective-permute-start(bf16[128,512]{1,0:T(8,128)(2,1)S(1)} %copy-done.5), channel_id=1, source_target_pairs={{0,4},{2,6},{4,0},{6,2},{1,5},{3,7},{5,1},{7,3},{8,12},{10,14},{12... | collective-permute-start | bytes 393224 | tf_op jit(solution)/shard_map/ppermute | solution.py:123
  23.7 16.7 %collective-permute-start = (bf16[128,512]{1,0:T(8,128)(2,1)S(1)}, bf16[128,512]{1,0:T(8,128)(2,1)S(1)}, u32[]{:S(2)}, u32[]{:S(2)}) collective-permute-start(bf16[128,512]{1,0:T(8,128)(2,1)S(1)} %copy-done.5), channel_id=1, source_target_pairs={{0,2},{2,4},{4,6},{6,0},{1,3},{3,5},{5,7},{7,1},{8,10},{10,12},{12... | collective-permute-start | bytes 393224 | tf_op jit(solution)/shard_map/ppermute | solution.py:123
  29.5 13.4 %collective-permute-start.2 = (bf16[128,512]{1,0:T(8,128)(2,1)S(1)}, bf16[128,512]{1,0:T(8,128)(2,1)S(1)}, u32[]{:S(2)}, u32[]{:S(2)}) collective-permute-start(bf16[128,512]{1,0:T(8,128)(2,1)S(1)} %copy-done.5), channel_id=1, source_target_pairs={{0,6},{2,0},{4,2},{6,4},{1,7},{3,1},{5,3},{7,5},{8,14},{10,8},{12,... | collective-permute-start | bytes 393224 | tf_op jit(solution)/shard_map/ppermute | solution.py:123
  53.3 36.2 %all-to-all-start.2 = ((bf16[8,4,32,512]{3,2,1,0:T(8,128)(2,1)}), bf16[8,4,32,512]{3,2,1,0:T(8,128)(2,1)S(1)}, u32[]{:S(2)}, u32[]{:S(2)}) async-start(bf16[8,4,32,512]{3,2,1,0:T(8,128)(2,1)} %reduce_sum.12), calls=%async_computation.2 | async-start | bytes 2097152 | tf_op jit(solution)/shard_map/all_to_all | solution.py:16
  60.6 3.8 %collective-permute-start.3 = (bf16[4,128,512]{2,1,0:T(8,128)(2,1)S(1)}, bf16[4,128,512]{2,1,0:T(8,128)(2,1)S(1)}, u32[]{:S(2)}, u32[]{:S(2)}) collective-permute-start(bf16[4,128,512]{2,1,0:T(8,128)(2,1)S(1)} %pad_maximum_fusion.2), channel_id=1, source_target_pairs={{0,1},{1,0},{2,3},{3,2},{4,5},{5,4},{6,7},{7,6},{8,9},{9,8},{10,11... | collective-permute-start | bytes 1572872 | tf_op jit(solution)/shard_map/ppermute | solution.py:133
  64.5 1.2 copy-start.6
  67.1 55.6 %copy-start.3 = (bf16[1024,1024]{1,0:T(8,128)(2,1)}, bf16[1024,1024]{1,0:T(8,128)(2,1)S(1)}, u32[]{:S(2)}) copy-start(bf16[1024,1024]{1,0:T(8,128)(2,1)S(1)} %convolution_convert_fusion.refs_0_) | copy-start | bytes 6291460

commit v3 on v2

--- a/solution.py
+++ b/solution.py
@@ -14,11 +14,6 @@
 
 def exchange(value, axes):
     return lax.all_to_all(value, axes, split_axis=0, concat_axis=0, tiled=True)
-
-
-def spread(value, axes, size):
-    copies = lax.optimization_barrier(jnp.broadcast_to(value[None], (size,) + value.shape))
-    return exchange(copies, axes)
 
 
 def lay_out(acts, cotangent):
@@ -41,59 +36,52 @@
             pl.BlockSpec((step, head), lambda i: (i, 0)),
         ],
         out_specs=pl.BlockSpec((NX, step, NODE * part + head), lambda i: (0, i, 0)),
-        out_shape=jax.ShapeDtypeStruct((NX, tok, NODE * part + head), jnp.bfloat16),
+        out_shape=pltpu.HBM((NX, tok, NODE * part + head), jnp.bfloat16),
         compiler_params=SMALL,
         cost_estimate=pl.CostEstimate(flops=0, bytes_accessed=2 * NX * tok * (NODE * part + head) * 2, transcendentals=0),
     )(acts, cotangent)
 
 
-def product(got, head, after):
+def product(got, head, core, received=None, after=()):
     tokens, width = got.shape
     part = (width - head) // NODE
     rows = part // NY
-
-    def kernel(acts_ref, cot_ref, *refs):
-        out_ref = refs[-1]
+    out = (NY, NZH, rows, head)
+    block = pl.BlockSpec((NY, 1, rows, head), lambda n, core_ref: (0, n, 0, 0))
+    more = [] if received is None else [received]
+
+    def kernel(core_ref, acts_ref, cot_ref, *refs):
         value = lax.dot_general(
             acts_ref[...], cot_ref[...], (((0,), (0,)), ((), ())), preferred_element_type=jnp.float32
-        )
-        out_ref[0, :, 0] = value.astype(jnp.bfloat16).reshape(NY, rows, head)
+        ).reshape(NY, rows, head)
+        if more:
+            value = value + refs[0][:, 0].astype(jnp.float32)
+        refs[-1][:, 0] = value.astype(jnp.bfloat16)
 
     return pl.pallas_call(
         kernel,
-        grid=(NODE,),
-        in_specs=[
-            pl.BlockSpec((tokens, part), lambda n: (0, n)),
-            pl.BlockSpec((tokens, head), lambda n: (0, NODE * part // head)),
-        ]
-        + [pl.BlockSpec(memory_space=pl.ANY)] * len(after),
-        out_specs=pl.BlockSpec((1, NY, 1, rows, head), lambda n: (n % NC, 0, n // NC, 0, 0)),
-        out_shape=jax.ShapeDtypeStruct((NC, NY, NZH, rows, head), jnp.bfloat16),
+        grid_spec=pltpu.PrefetchScalarGridSpec(
+            num_scalar_prefetch=1,
+            grid=(NZH,),
+            in_specs=[
+                pl.BlockSpec((tokens, part), lambda n, core_ref: (0, n * NC + core_ref[0])),
+                pl.BlockSpec((tokens, head), lambda n, core_ref: (0, NODE * part // head)),
+            ]
+            + [block] * len(more)
+            + [pl.BlockSpec(memory_space=pl.ANY)] * len(after),
+            out_specs=block,
+        ),
+        out_shape=pltpu.HBM(out, jnp.bfloat16) if more else jax.ShapeDtypeStruct(out, jnp.bfloat16),
         compiler_params=SMALL,
         cost_estimate=pl.CostEstimate(
-            flops=2 * tokens * NODE * part * head,
-            bytes_accessed=(tokens * width + NODE * part * head) * 2,
+            flops=tokens * NODE * part * head,
+            bytes_accessed=tokens * width * 2,
             transcendentals=0,
         ),
-    )(got, got, *after)
-
-
-def add(value):
-    return jnp.sum(value.astype(jnp.float32), axis=0).astype(jnp.bfloat16)
-
-
-def add_copies(value, copies, axis, after=()):
-    shape = value.shape[1:]
-    out = shape[:axis] + (copies,) + shape[axis:]
-
-    def kernel(value_ref, *refs):
-        total = value_ref[0].astype(jnp.float32)
-        for i in range(1, value.shape[0]):
-            total = total + value_ref[i].astype(jnp.float32)
-        total = total.astype(jnp.bfloat16)
-        for i in range(copies):
-            refs[-1][(slice(None),) * axis + (i,)] = total
-
+    )(core, got, got, *more, *after)
+
+
+def small_kernel(kernel, out, value, after=()):
     return pl.pallas_call(
         kernel,
         in_specs=[pl.BlockSpec(memory_space=pltpu.VMEM)] + [pl.BlockSpec(memory_space=pl.ANY)] * len(after),
@@ -104,6 +92,62 @@
     )(value, *after)
 
 
+def total_of(ref, index):
+    total = ref[(0,) + index].astype(jnp.float32)
+    for i in range(1, ref.shape[0]):
+        total = total + ref[(i,) + index].astype(jnp.float32)
+    return total.astype(jnp.bfloat16)
+
+
+PIECE, LANES = 16, 128
+
+
+def pieces(rows, head):
+    whole = (rows // PIECE) * (head // LANES)
+    each = -(-whole // NZL)
+    return each, [
+        (p // each, p % each * PIECE, p % (rows // PIECE) * PIECE, p // (rows // PIECE) * LANES) for p in range(whole)
+    ]
+
+
+def sum_y(value, after):
+    ny, nzh, rows, head = value.shape
+    each, where = pieces(rows, head)
+
+    def kernel(value_ref, *refs):
+        out_ref = refs[-1]
+        for zh in range(nzh):
+            out_ref[zh, NZL - 1] = jnp.zeros(out_ref.shape[2:], jnp.bfloat16)
+            for zl, slot, row, column in where:
+                out_ref[zh, zl, slot : slot + PIECE] = total_of(
+                    value_ref, (zh, slice(row, row + PIECE), slice(column, column + LANES))
+                )
+
+    return small_kernel(kernel, (nzh, NZL, each * PIECE, LANES), value, after)
+
+
+def sum_z(value):
+    def kernel(value_ref, out_ref):
+        total = total_of(value_ref, ())
+        for i in range(NY * NZL):
+            out_ref[i] = total
+
+    return small_kernel(kernel, (NY * NZL,) + value.shape[1:], value)
+
+
+def join(value, rows, head):
+    _, where = pieces(rows, head)
+
+    def kernel(value_ref, out_ref):
+        for y in range(NY):
+            for zl, slot, row, column in where:
+                piece = value_ref[y, zl, slot : slot + PIECE]
+                for x in range(NX):
+                    out_ref[x, y, row : row + PIECE, column : column + LANES] = piece
+
+    return small_kernel(kernel, (NX, NY, rows, head), value)
+
+
 def input_gradient(peers, w_values, w_scales):
     head = w_values.shape[1]
     blocks = w_values.shape[0] // 128
@@ -143,19 +187,22 @@
     rows = part // NY
     factor = (tok * NY * NX * NZL * NZH * NC) ** (-0.5)
 
-    got = exchange(lay_out(acts, cotangent), "x")
+    core = lax.axis_index("c")[None]
+    got = exchange(lay_out(acts, cotangent), "x").reshape(NX * tok, NODE * part + head)
     mine = gather_zh(cotangent)
-    partial = product(got.reshape(NX * tok, NODE * part + head), head, mine[1:])
-    chip = add(exchange(partial, "c"))
+    theirs = product(got, head, 1 - core, after=mine[1:])
+    chip = product(got, head, core, received=lax.ppermute(theirs, "c", [(0, 1), (1, 0)]))
 
     over_y = exchange(chip, "y")
     peers = gather_node(mine).reshape(NODE * tok, head)
     input_grad = input_gradient(peers, w_values, w_scales)
 
-    slots = add_copies(over_y, NZL, 1, [input_grad]).reshape(NZH * NZL, rows, head)
-    total = add_copies(exchange(slots, ("zh", "zl")), NY, 0)
-    back = exchange(total, "y").reshape(part, head)
-    full = spread(back, "x", NX).reshape(owned, head)
+    slots = sum_y(over_y, [input_grad])
+    slots = slots.reshape((NZH * NZL,) + slots.shape[2:])
+    copies = sum_z(exchange(slots, ("zh", "zl")))
+    back = exchange(copies, ("y", "zl"))
+    back = join(back.reshape((NY, NZL) + back.shape[1:]), rows, head)
+    full = exchange(back, "x").reshape(owned, head)
     return (input_grad, full.astype(jnp.float32) * factor)
 
 

time: 156 us -> 147 us (0.942)
  the two profiles are of different devices: /device:TPU:64 before, /device:TPU:72 now
where the time goes in v3:
time: 147 us; the launch traced here: 146 us
  blocking collectives  57.7 us (39%)
  starting transfers between devices  39.5 us (27%)
  waiting for transfers between devices  34.5 us (23%)
  Pallas kernels  6.47 us (4%)
  local copies, waits for them, and re-layouts  3.74 us (3%)
  other arithmetic  1.95 us (1%)
    all_to_all x3, blocking collectives, exchange(): return lax.all_to_all(value, axes, split_axis=0, concat_axis=0, tiled=True)  57.7 us
    ppermute x3, starting transfers between devices, gather_zh(): lax.ppermute(cotangent, 'zh', [(i, (i + k) % NZH) for i in range(NZH)])  23.7 us
    all_to_all x2, waiting for transfers between devices, exchange(): return lax.all_to_all(value, axes, split_axis=0, concat_axis=0, tiled=True)  20.8 us
    all_to_all x2, starting transfers between devices, exchange(): return lax.all_to_all(value, axes, split_axis=0, concat_axis=0, tiled=True)  12 us
    ppermute x3, waiting for transfers between devices, gather_zh(): lax.ppermute(cotangent, 'zh', [(i, (i + k) % NZH) for i in range(NZH)])  9.29 us
    pallas_call x2, Pallas kernels, product(): pl.pallas_call(kernel, grid_spec=pltpu.PrefetchScalarGridSpec(num_scalar_...  4.11 us
    unnamed x12, local copies, waits for them, and re-layouts  3.52 us
  transfers between devices with their start and end apart: 7, of which 6 were waited for; matrix products, arithmetic and copies ran while one was open for 1% of the time, Pallas kernels for 0%

profile of v3, /device:TPU:72, one launch (start us, length us, event | category | flops | bytes accessed | tf_op | source)
XLA Modules:
  0.0 146.0 jit_solution(6276148484105159348)
XLA Ops:
  0.7 1.6 %copy-done.1 = bf16[128,8192]{1,0:T(8,128)(2,1)S(1)} copy-done((bf16[128,8192]{1,0:T(8,128)(2,1)S(1)}, bf16[128,8192]{1,0:T(8,128)(2,1)}, u32[]{:S(2)}) %copy-start.1) | copy-done | bytes 2097176
  2.2 0.9 copy-done.3
  3.1 2.0 %shard_map.59 = bf16[4,128,2560]{2,1,0:T(8,128)(2,1)} custom-call(bf16[128,8192]{1,0:T(8,128)(2,1)S(1)} %copy-done.1, bf16[128,512]{1,0:T(8,128)(2,1)S(1)} %copy-done.3), custom_call_target="tpu_custom_call" | custom-call | bytes 5242880 | tf_op jit(solution)/shard_map/pallas_call | solution.py:31
  5.2 4.4 %all-to-all-start = ((bf16[4,128,2560]{2,1,0:T(8,128)(2,1)}), bf16[4,128,2560]{2,1,0:T(8,128)(2,1)S(1)}, u32[]{:S(2)}, u32[]{:S(2)}) async-start(bf16[4,128,2560]{2,1,0:T(8,128)(2,1)} %shard_map.59), calls=%async_computation | async-start | bytes 5242880 | tf_op jit(solution)/shard_map/all_to_all | solution.py:16
  9.6 13.7 %collective-permute-start.2 = (bf16[128,512]{1,0:T(8,128)(2,1)S(1)}, bf16[128,512]{1,0:T(8,128)(2,1)S(1)}, u32[]{:S(2)}, u32[]{:S(2)}) collective-permute-start(bf16[128,512]{1,0:T(8,128)(2,1)S(1)} %copy-done.4), channel_id=1, source_target_pairs={{0,6},{2,0},{4,2},{6,4},{1,7},{3,1},{5,3},{7,5},{8,14},{10,8},{12,... | collective-permute-start | bytes 393224 | tf_op jit(solution)/shard_map/ppermute | solution.py:167
  23.3 2.5 %collective-permute-start.1 = (bf16[128,512]{1,0:T(8,128)(2,1)S(1)}, bf16[128,512]{1,0:T(8,128)(2,1)S(1)}, u32[]{:S(2)}, u32[]{:S(2)}) collective-permute-start(bf16[128,512]{1,0:T(8,128)(2,1)S(1)} %copy-done.4), channel_id=1, source_target_pairs={{0,4},{2,6},{4,0},{6,2},{1,5},{3,7},{5,1},{7,3},{8,12},{10,14},{12... | collective-permute-start | bytes 393224 | tf_op jit(solution)/shard_map/ppermute | solution.py:167
  25.8 7.5 %collective-permute-start = (bf16[128,512]{1,0:T(8,128)(2,1)S(1)}, bf16[128,512]{1,0:T(8,128)(2,1)S(1)}, u32[]{:S(2)}, u32[]{:S(2)}) collective-permute-start(bf16[128,512]{1,0:T(8,128)(2,1)S(1)} %copy-done.4), channel_id=1, source_target_pairs={{0,2},{2,4},{4,6},{6,0},{1,3},{3,5},{5,7},{7,1},{8,10},{10,12},{12... | collective-permute-start | bytes 393224 | tf_op jit(solution)/shard_map/ppermute | solution.py:167
  33.3 2.3 %collective-permute-done.2.refs_2_ = bf16[128,512]{1,0:T(8,128)(2,1)S(1)} collective-permute-done((bf16[128,512]{1,0:T(8,128)(2,1)S(1)}, bf16[128,512]{1,0:T(8,128)(2,1)S(1)}, u32[]{:S(2)}, u32[]{:S(2)}) %collective-permute-start.2) | collective-permute-done | bytes 131104 | tf_op jit(solution)/shard_map/ppermute | solution.py:167
  35.7 6.4 %collective-permute-done.1.refs_1_ = bf16[128,512]{1,0:T(8,128)(2,1)S(1)} collective-permute-done((bf16[128,512]{1,0:T(8,128)(2,1)S(1)}, bf16[128,512]{1,0:T(8,128)(2,1)S(1)}, u32[]{:S(2)}, u32[]{:S(2)}) %collective-permute-start.1) | collective-permute-done | bytes 131104 | tf_op jit(solution)/shard_map/ppermute | solution.py:167
  42.0 0.6 collective-permute-done.refs_0_
  42.6 1.5 %shard_map.60 = bf16[8,4,32,512]{3,2,1,0:T(8,128)(2,1)S(1)} custom-call(s32[1]{0:T(128)S(6)} %sub.15.core_ref, bf16[512,2560]{1,0:T(8,128)(2,1)S(1)} %bitcast.17, bf16[512,2560]{1,0:T(8,128)(2,1)S(1)} %bitcast.18, bf16[128,512]{1,0:T(8,128)(2,1)S(1)} %collective-permute-done.refs_0_, bf16[128,512]{1,0:T(8,128)(2,1)S(1)} %collective-permute-done.1.refs_1_, ...), custom_call_target="tpu_custom_call" | custom-call | flops 536870912 | bytes 2621440 | tf_op jit(solution)/shard_map/pallas_call | solution.py:61
  44.2 1.9 %collective-permute-start.4 = (bf16[8,4,32,512]{3,2,1,0:T(8,128)(2,1)S(1)}, bf16[8,4,32,512]{3,2,1,0:T(8,128)(2,1)S(1)}, u32[]{:S(2)}, u32[]{:S(2)}) collective-permute-start(bf16[8,4,32,512]{3,2,1,0:T(8,128)(2,1)S(1)} %shard_map.60), channel_id=1, source_target_pairs={{0,1},{1,0},{2,3},{3,2},{4,5},{5,4},{6,7},{7,6},{8,9},{9,8},{10,11... | collective-permute-start | bytes 3145736 | tf_op jit(solution)/shard_map/ppermute | solution.py:194
  46.1 2.6 %collective-permute-done.4.refs_0_ = bf16[8,4,32,512]{3,2,1,0:T(8,128)(2,1)S(1)} collective-permute-done((bf16[8,4,32,512]{3,2,1,0:T(8,128)(2,1)S(1)}, bf16[8,4,32,512]{3,2,1,0:T(8,128)(2,1)S(1)}, u32[]{:S(2)}, u32[]{:S(2)}) %collective-permute-start.4) | collective-permute-done | bytes 1048608 | tf_op jit(solution)/shard_map/ppermute | solution.py:194
  48.7 2.6 %shard_map.61 = bf16[8,4,32,512]{3,2,1,0:T(8,128)(2,1)} custom-call(s32[1]{0:T(128)} %bitcast.8.core_ref, bf16[512,2560]{1,0:T(8,128)(2,1)S(1)} %bitcast.19, bf16[512,2560]{1,0:T(8,128)(2,1)S(1)} %bitcast.20, bf16[8,4,32,512]{3,2,1,0:T(8,128)(2,1)S(1)} %collective-permute-done.4.refs_0_), custom_call_target="tpu_custom_call" | custom-call | flops 536870912 | bytes 2621440 | tf_op jit(solution)/shard_map/pallas_call | solution.py:61
  51.3 7.5 %all-to-all-start.1 = ((bf16[8,4,32,512]{3,2,1,0:T(8,128)(2,1)}), bf16[8,4,32,512]{3,2,1,0:T(8,128)(2,1)S(1)}, u32[]{:S(2)}, u32[]{:S(2)}) async-start(bf16[8,4,32,512]{3,2,1,0:T(8,128)(2,1)} %shard_map.61), calls=%async_computation.1 | async-start | bytes 2097152 | tf_op jit(solution)/shard_map/all_to_all | solution.py:16
  58.9 0.1 pad_maximum_fusion.1
  59.0 0.1 pad_maximum_fusion.2
  59.1 1.9 %collective-permute-start.3 = (bf16[4,128,512]{2,1,0:T(8,128)(2,1)S(1)}, bf16[4,128,512]{2,1,0:T(8,128)(2,1)S(1)}, u32[]{:S(2)}, u32[]{:S(2)}) collective-permute-start(bf16[4,128,512]{2,1,0:T(8,128)(2,1)S(1)} %pad_maximum_fusion.2), channel_id=1, source_target_pairs={{0,1},{1,0},{2,3},{3,2},{4,5},{5,4},{6,7},{7,6},{8,9},{9,8},{10,11... | collective-permute-start | bytes 1572872 | tf_op jit(solution)/shard_map/ppermute | solution.py:177
  61.0 0.1 broadcast_bitcast_fusion
  61.1 1.8 %collective-permute-done.3 = bf16[4,128,512]{2,1,0:T(8,128)(2,1)S(1)} collective-permute-done((bf16[4,128,512]{2,1,0:T(8,128)(2,1)S(1)}, bf16[4,128,512]{2,1,0:T(8,128)(2,1)S(1)}, u32[]{:S(2)}, u32[]{:S(2)}) %collective-permute-start.3) | collective-permute-done | bytes 524320 | tf_op jit(solution)/shard_map/ppermute | solution.py:177
  62.9 0.1 select_bitcast_fusion.1
  63.0 0.1 pad_maximum_fusion
  63.1 0.1 copy.6
  63.2 1.0 copy-done.5
  64.2 1.4 convolution_convert_fusion.refs_0_
  65.6 20.8 %all-to-all-done.1.value_ref = bf16[8,4,32,512]{3,2,1,0:T(8,128)(2,1)S(1)} async-done(((bf16[8,4,32,512]{3,2,1,0:T(8,128)(2,1)}), bf16[8,4,32,512]{3,2,1,0:T(8,128)(2,1)S(1)}, u32[]{:S(2)}, u32[]{:S(2)}) %all-to-all-start.1) | async-done | bytes 1048608 | tf_op jit(solution)/shard_map/all_to_all | solution.py:16
  86.4 0.1 shard_map.62
  86.6 24.6 %all_to_all.25.value_ref = bf16[12,48,128]{2,1,0:T(8,128)(2,1)S(1)} all-to-all(bf16[12,48,128]{2,1,0:T(8,128)(2,1)S(1)} %bitcast.22), channel_id=1, replica_groups=mesh['y'=8,'x'=4,'zl'=3,'zh'=4,'c'=2] {'zh','zl'}, dimensions={0} | all-to-all | bytes 294912 | tf_op jit(solution)/shard_map/all_to_all | solution.py:16
  111.2 15.7 %all_to_all.26 = bf16[24,48,128]{2,1,0:T(8,128)(2,1)S(1)} all-to-all(bf16[24,48,128]{2,1,0:T(8,128)(2,1)S(1)} %shard_map.63), channel_id=1, replica_groups=mesh['y'=8,'x'=4,'zl'=3,'zh'=4,'c'=2] {'y','zl'}, dimensions={0} | all-to-all | bytes 589824 | tf_op jit(solution)/shard_map/all_to_all | solution.py:16
  126.9 0.1 shard_map.64
  127.1 17.3 %all_to_all.27 = bf16[4,8,32,512]{3,2,1,0:T(8,128)(2,1)S(1)} all-to-all(bf16[4,8,32,512]{3,2,1,0:T(8,128)(2,1)S(1)} %shard_map.64), channel_id=1, replica_groups=mesh['y'=8,'x'=4,'zl'=3,'zh'=4,'c'=2] {'x'}, dimensions={0} | all-to-all | bytes 2097152 | tf_op jit(solution)/shard_map/all_to_all | solution.py:16
  144.4 1.6 %convert_multiply_fusion = f32[4,8,32,512]{3,2,1,0:T(8,128)} fusion(bf16[4,8,32,512]{3,2,1,0:T(8,128)(2,1)S(1)} %all_to_all.27), kind=kLoop, calls=%fused_computation | loop fusion | flops 1048576 | bytes 3145728 | tf_op jit(solution)/shard_map/mul | solution.py:206
  (12 shorter events, 0.1 us)
Async XLA Ops:
  0.6 60.4 %copy-start = (f32[8]{0:T(128)S(1)}, f32[8]{0:T(128)}, u32[]{:S(2)}) copy-start(f32[8]{0:T(128)} %param.7) | copy-start | bytes 100
  0.6 1.6 %copy-start.1 = (bf16[128,8192]{1,0:T(8,128)(2,1)S(1)}, bf16[128,8192]{1,0:T(8,128)(2,1)}, u32[]{:S(2)}) copy-start(bf16[128,8192]{1,0:T(8,128)(2,1)} %acts_ref.1) | copy-start | bytes 6291460
  2.2 0.9 copy-start.3
  5.2 4.4 %copy-start.4 = (bf16[128,512]{1,0:T(8,128)(2,1)S(1)}, bf16[128,512]{1,0:T(8,128)(2,1)}, u32[]{:S(2)}) copy-start(bf16[128,512]{1,0:T(8,128)(2,1)} %cot_ref.1) | copy-start | bytes 393220
  5.2 37.4 %all-to-all-start = ((bf16[4,128,2560]{2,1,0:T(8,128)(2,1)}), bf16[4,128,2560]{2,1,0:T(8,128)(2,1)S(1)}, u32[]{:S(2)}, u32[]{:S(2)}) async-start(bf16[4,128,2560]{2,1,0:T(8,128)(2,1)} %shard_map.59), calls=%async_computation | async-start | bytes 5242880 | tf_op jit(solution)/shard_map/all_to_all | solution.py:16
  9.6 26.0 %collective-permute-start.2 = (bf16[128,512]{1,0:T(8,128)(2,1)S(1)}, bf16[128,512]{1,0:T(8,128)(2,1)S(1)}, u32[]{:S(2)}, u32[]{:S(2)}) collective-permute-start(bf16[128,512]{1,0:T(8,128)(2,1)S(1)} %copy-done.4), channel_id=1, source_target_pairs={{0,6},{2,0},{4,2},{6,4},{1,7},{3,1},{5,3},{7,5},{8,14},{10,8},{12,... | collective-permute-start | bytes 393224 | tf_op jit(solution)/shard_map/ppermute | solution.py:167
  23.3 18.7 %collective-permute-start.1 = (bf16[128,512]{1,0:T(8,128)(2,1)S(1)}, bf16[128,512]{1,0:T(8,128)(2,1)S(1)}, u32[]{:S(2)}, u32[]{:S(2)}) collective-permute-start(bf16[128,512]{1,0:T(8,128)(2,1)S(1)} %copy-done.4), channel_id=1, source_target_pairs={{0,4},{2,6},{4,0},{6,2},{1,5},{3,7},{5,1},{7,3},{8,12},{10,14},{12... | collective-permute-start | bytes 393224 | tf_op jit(solution)/shard_map/ppermute | solution.py:167
  25.8 16.8 %collective-permute-start = (bf16[128,512]{1,0:T(8,128)(2,1)S(1)}, bf16[128,512]{1,0:T(8,128)(2,1)S(1)}, u32[]{:S(2)}, u32[]{:S(2)}) collective-permute-start(bf16[128,512]{1,0:T(8,128)(2,1)S(1)} %copy-done.4), channel_id=1, source_target_pairs={{0,2},{2,4},{4,6},{6,0},{1,3},{3,5},{5,7},{7,1},{8,10},{10,12},{12... | collective-permute-start | bytes 393224 | tf_op jit(solution)/shard_map/ppermute | solution.py:167
  44.2 4.6 %collective-permute-start.4 = (bf16[8,4,32,512]{3,2,1,0:T(8,128)(2,1)S(1)}, bf16[8,4,32,512]{3,2,1,0:T(8,128)(2,1)S(1)}, u32[]{:S(2)}, u32[]{:S(2)}) collective-permute-start(bf16[8,4,32,512]{3,2,1,0:T(8,128)(2,1)S(1)} %shard_map.60), channel_id=1, source_target_pairs={{0,1},{1,0},{2,3},{3,2},{4,5},{5,4},{6,7},{7,6},{8,9},{9,8},{10,11... | collective-permute-start | bytes 3145736 | tf_op jit(solution)/shard_map/ppermute | solution.py:194
  51.3 35.1 %all-to-all-start.1 = ((bf16[8,4,32,512]{3,2,1,0:T(8,128)(2,1)}), bf16[8,4,32,512]{3,2,1,0:T(8,128)(2,1)S(1)}, u32[]{:S(2)}, u32[]{:S(2)}) async-start(bf16[8,4,32,512]{3,2,1,0:T(8,128)(2,1)} %shard_map.61), calls=%async_computation.1 | async-start | bytes 2097152 | tf_op jit(solution)/shard_map/all_to_all | solution.py:16
  59.1 3.8 %collective-permute-start.3 = (bf16[4,128,512]{2,1,0:T(8,128)(2,1)S(1)}, bf16[4,128,512]{2,1,0:T(8,128)(2,1)S(1)}, u32[]{:S(2)}, u32[]{:S(2)}) collective-permute-start(bf16[4,128,512]{2,1,0:T(8,128)(2,1)S(1)} %pad_maximum_fusion.2), channel_id=1, source_target_pairs={{0,1},{1,0},{2,3},{3,2},{4,5},{5,4},{6,7},{7,6},{8,9},{9,8},{10,11... | collective-permute-start | bytes 1572872 | tf_op jit(solution)/shard_map/ppermute | solution.py:177
  63.0 1.2 copy-start.5
  65.6 61.3 %copy-start.2 = (bf16[1024,1024]{1,0:T(8,128)(2,1)}, bf16[1024,1024]{1,0:T(8,128)(2,1)S(1)}, u32[]{:S(2)}) copy-start(bf16[1024,1024]{1,0:T(8,128)(2,1)S(1)} %convolution_convert_fusion.refs_0_) | copy-start | bytes 6291460

commit v4 on v3

--- a/solution.py
+++ b/solution.py
@@ -6,9 +6,11 @@
 from jax.sharding import Mesh
 from jax.sharding import PartitionSpec as P
 
-AXES = ("y", "x", "zl", "zh", "c")
-NY, NX, NZL, NZH, NC = SIZES = (8, 4, 3, 4, 2)
+AXES = ("yh", "yl", "x", "zl", "zh", "c")
+NYH, NYL, NX, NZL, NZH, NC = SIZES = (4, 2, 4, 3, 4, 2)
 NODE = NZH * NC
+NEAR = NX * NYL
+LARGE = pltpu.CompilerParams(vmem_limit_bytes=60 * 2**20)
 SMALL = pltpu.CompilerParams(vmem_limit_bytes=12 * 2**20)
 
 
@@ -19,15 +21,18 @@
 def lay_out(acts, cotangent):
     tok, width = acts.shape
     head = cotangent.shape[1]
-    part = width // (NODE * NX)
+    part = width // (NODE * NEAR)
     step = 32
 
     def kernel(acts_ref, cot_ref, out_ref):
-        for x in range(NX):
-            for n in range(NODE):
-                out_ref[x, :, n * part : (n + 1) * part] = acts_ref[:, pl.ds((n * NX + x) * part, part)]
-            out_ref[x, :, NODE * part :] = cot_ref[...]
-
+        for s in range(NEAR):
+            for c in range(NC):
+                for zh in range(NZH):
+                    to, source = (c * NZH + zh) * part, ((zh * NC + c) * NEAR + s) * part
+                    out_ref[s, :, to : to + part] = acts_ref[:, source : source + part]
+            out_ref[s, :, NODE * part :] = cot_ref[...]
+
+    out = (NEAR, tok, NODE * part + head)
     return pl.pallas_call(
         kernel,
         grid=(tok // step,),
@@ -35,36 +40,41 @@
             pl.BlockSpec((step, width), lambda i: (i, 0)),
             pl.BlockSpec((step, head), lambda i: (i, 0)),
         ],
-        out_specs=pl.BlockSpec((NX, step, NODE * part + head), lambda i: (0, i, 0)),
-        out_shape=pltpu.HBM((NX, tok, NODE * part + head), jnp.bfloat16),
-        compiler_params=SMALL,
-        cost_estimate=pl.CostEstimate(flops=0, bytes_accessed=2 * NX * tok * (NODE * part + head) * 2, transcendentals=0),
+        out_specs=pl.BlockSpec((NEAR, step, out[2]), lambda i: (0, i, 0)),
+        out_shape=pltpu.HBM(out, jnp.bfloat16),
+        compiler_params=LARGE,
+        cost_estimate=pl.CostEstimate(flops=0, bytes_accessed=4 * NEAR * tok * out[2], transcendentals=0),
     )(acts, cotangent)
 
 
 def product(got, head, core, received=None, after=()):
     tokens, width = got.shape
     part = (width - head) // NODE
-    rows = part // NY
-    out = (NY, NZH, rows, head)
-    block = pl.BlockSpec((NY, 1, rows, head), lambda n, core_ref: (0, n, 0, 0))
+    rows = part // NYH
+    group = 2
+    out = (NYH, NZH, rows, head)
+    block = pl.BlockSpec((NYH, group, rows, head), lambda n, core_ref: (0, n, 0, 0))
     more = [] if received is None else [received]
 
     def kernel(core_ref, acts_ref, cot_ref, *refs):
         value = lax.dot_general(
             acts_ref[...], cot_ref[...], (((0,), (0,)), ((), ())), preferred_element_type=jnp.float32
-        ).reshape(NY, rows, head)
-        if more:
-            value = value + refs[0][:, 0].astype(jnp.float32)
-        refs[-1][:, 0] = value.astype(jnp.bfloat16)
+        )
+        for zh in range(group):
+            for y in range(NYH):
+                first = (zh * NYH + y) * rows
+                piece = value[first : first + rows]
+                if more:
+                    piece = piece + refs[0][y, zh].astype(jnp.float32)
+                refs[-1][y, zh] = piece.astype(jnp.bfloat16)
 
     return pl.pallas_call(
         kernel,
         grid_spec=pltpu.PrefetchScalarGridSpec(
             num_scalar_prefetch=1,
-            grid=(NZH,),
+            grid=(NZH // group,),
             in_specs=[
-                pl.BlockSpec((tokens, part), lambda n, core_ref: (0, n * NC + core_ref[0])),
+                pl.BlockSpec((tokens, group * part), lambda n, core_ref: (0, core_ref[0] * (NZH // group) + n)),
                 pl.BlockSpec((tokens, head), lambda n, core_ref: (0, NODE * part // head)),
             ]
             + [block] * len(more)
@@ -129,23 +139,23 @@
 def sum_z(value):
     def kernel(value_ref, out_ref):
         total = total_of(value_ref, ())
-        for i in range(NY * NZL):
+        for i in range(NYH * NZL):
             out_ref[i] = total
 
-    return small_kernel(kernel, (NY * NZL,) + value.shape[1:], value)
+    return small_kernel(kernel, (NYH * NZL,) + value.shape[1:], value)
 
 
 def join(value, rows, head):
     _, where = pieces(rows, head)
 
     def kernel(value_ref, out_ref):
-        for y in range(NY):
+        for y in range(NYH):
             for zl, slot, row, column in where:
                 piece = value_ref[y, zl, slot : slot + PIECE]
-                for x in range(NX):
-                    out_ref[x, y, row : row + PIECE, column : column + LANES] = piece
-
-    return small_kernel(kernel, (NX, NY, rows, head), value)
+                for s in range(NEAR):
+                    out_ref[s, y, row : row + PIECE, column : column + LANES] = piece
+
+    return small_kernel(kernel, (NEAR, NYH, rows, head), value)
 
 
 def input_gradient(peers, w_values, w_scales):
@@ -183,32 +193,32 @@
     tok, width = acts.shape
     head = cotangent.shape[1]
     owned = width // NODE
-    part = owned // NX
-    rows = part // NY
-    factor = (tok * NY * NX * NZL * NZH * NC) ** (-0.5)
+    part = owned // NEAR
+    rows = part // NYH
+    factor = (tok * NYH * NYL * NX * NZL * NZH * NC) ** (-0.5)
 
     core = lax.axis_index("c")[None]
-    got = exchange(lay_out(acts, cotangent), "x").reshape(NX * tok, NODE * part + head)
+    got = exchange(lay_out(acts, cotangent), ("x", "yl")).reshape(NEAR * tok, NODE * part + head)
     mine = gather_zh(cotangent)
     theirs = product(got, head, 1 - core, after=mine[1:])
     chip = product(got, head, core, received=lax.ppermute(theirs, "c", [(0, 1), (1, 0)]))
 
-    over_y = exchange(chip, "y")
+    over_y = exchange(chip, "yh")
     peers = gather_node(mine).reshape(NODE * tok, head)
     input_grad = input_gradient(peers, w_values, w_scales)
 
     slots = sum_y(over_y, [input_grad])
     slots = slots.reshape((NZH * NZL,) + slots.shape[2:])
     copies = sum_z(exchange(slots, ("zh", "zl")))
-    back = exchange(copies, ("y", "zl"))
-    back = join(back.reshape((NY, NZL) + back.shape[1:]), rows, head)
-    full = exchange(back, "x").reshape(owned, head)
+    back = exchange(copies, ("yh", "zl"))
+    back = join(back.reshape((NYH, NZL) + back.shape[1:]), rows, head)
+    full = exchange(back, ("x", "yl")).reshape(owned, head)
     return (input_grad, full.astype(jnp.float32) * factor)
 
 
 def solution(mesh):
     fine = Mesh(mesh.devices.reshape(SIZES), AXES)
-    dp, node = ("y", "x", "zl"), ("zh", "c")
+    dp, node = ("yh", "yl", "x", "zl"), ("zh", "c")
     placed = (P(dp + node, None), P(dp + node, None), P(node, None), P(node))
     return jax.shard_map(
         local,

time: 147 us -> 140 us (0.952)
  the two profiles are of different devices: /device:TPU:72 before, /device:TPU:8 now
where the time goes in v4:
time: 140 us
  blocking collectives  58.1 us (42%)
  starting transfers between devices  39.6 us (28%)
  waiting for transfers between devices  26 us (19%)
  Pallas kernels  7.48 us (5%)
  other arithmetic  4.81 us (3%)
    all_to_all x3, blocking collectives, exchange(): return lax.all_to_all(value, axes, split_axis=0, concat_axis=0, tiled=True)  58.1 us
    all_to_all x2, starting transfers between devices, exchange(): return lax.all_to_all(value, axes, split_axis=0, concat_axis=0, tiled=True)  19.2 us
    ppermute x3, starting transfers between devices, gather_zh(): lax.ppermute(cotangent, 'zh', [(i, (i + k) % NZH) for i in range(NZH)])  16.1 us
    all_to_all x2, waiting for transfers between devices, exchange(): return lax.all_to_all(value, axes, split_axis=0, concat_axis=0, tiled=True)  15.8 us
    ppermute x3, waiting for transfers between devices, gather_zh(): lax.ppermute(cotangent, 'zh', [(i, (i + k) % NZH) for i in range(NZH)])  10.3 us
    pallas_call x1, Pallas kernels, lay_out(): pl.pallas_call(kernel, grid=(tok // step,), in_specs=[pl.BlockSpec((step,...  4.17 us
    pallas_call x2, Pallas kernels, product(): pl.pallas_call(kernel, grid_spec=pltpu.PrefetchScalarGridSpec(num_scalar_...  3.05 us
  transfers between devices with their start and end apart: 7, of which 5 were waited for; matrix products, arithmetic and copies ran while one was open for 3% of the time, Pallas kernels for 1%

profile of v4, /device:TPU:8, one launch (start us, length us, event | category | flops | bytes accessed | tf_op | source)
XLA Modules:
  0.0 139.6 jit_solution(2991984883888019152)
XLA Ops:
  0.6 0.0 copy-start
  0.6 4.2 %shard_map.59 = bf16[8,128,1536]{2,1,0:T(8,128)(2,1)} custom-call(bf16[128,8192]{1,0:T(8,128)(2,1)} %acts_ref.1, bf16[128,512]{1,0:T(8,128)(2,1)} %cot_ref.1), custom_call_target="tpu_custom_call" | custom-call | bytes 6291456 | tf_op jit(solution)/shard_map/pallas_call | solution.py:36
  4.8 13.0 %all-to-all-start = ((bf16[8,128,1536]{2,1,0:T(8,128)(2,1)}), bf16[8,128,1536]{2,1,0:T(8,128)(2,1)S(1)}, u32[]{:S(2)}, u32[]{:S(2)}) async-start(bf16[8,128,1536]{2,1,0:T(8,128)(2,1)} %shard_map.59), calls=%async_computation | async-start | bytes 6291456 | tf_op jit(solution)/shard_map/all_to_all | solution.py:18
  17.8 7.3 %collective-permute-start.2 = (bf16[128,512]{1,0:T(8,128)(2,1)}, bf16[128,512]{1,0:T(8,128)(2,1)S(1)}, u32[]{:S(2)}, u32[]{:S(2)}) collective-permute-start(bf16[128,512]{1,0:T(8,128)(2,1)} %cot_ref.1), channel_id=1, source_target_pairs={{0,6},{2,0},{4,2},{6,4},{1,7},{3,1},{5,3},{7,5},{8,14},{10,8},{12,... | collective-permute-start | bytes 393224 | tf_op jit(solution)/shard_map/ppermute | solution.py:177
  25.1 2.5 %collective-permute-start.1 = (bf16[128,512]{1,0:T(8,128)(2,1)}, bf16[128,512]{1,0:T(8,128)(2,1)S(1)}, u32[]{:S(2)}, u32[]{:S(2)}) collective-permute-start(bf16[128,512]{1,0:T(8,128)(2,1)} %cot_ref.1), channel_id=1, source_target_pairs={{0,4},{2,6},{4,0},{6,2},{1,5},{3,7},{5,1},{7,3},{8,12},{10,14},{12... | collective-permute-start | bytes 393224 | tf_op jit(solution)/shard_map/ppermute | solution.py:177
  27.6 6.3 %collective-permute-start = (bf16[128,512]{1,0:T(8,128)(2,1)}, bf16[128,512]{1,0:T(8,128)(2,1)S(1)}, u32[]{:S(2)}, u32[]{:S(2)}) collective-permute-start(bf16[128,512]{1,0:T(8,128)(2,1)} %cot_ref.1), channel_id=1, source_target_pairs={{0,2},{2,4},{4,6},{6,0},{1,3},{3,5},{5,7},{7,1},{8,10},{10,12},{12... | collective-permute-start | bytes 393224 | tf_op jit(solution)/shard_map/ppermute | solution.py:177
  34.1 7.7 %collective-permute-done.2.refs_2_ = bf16[128,512]{1,0:T(8,128)(2,1)S(1)} collective-permute-done((bf16[128,512]{1,0:T(8,128)(2,1)}, bf16[128,512]{1,0:T(8,128)(2,1)S(1)}, u32[]{:S(2)}, u32[]{:S(2)}) %collective-permute-start.2) | collective-permute-done | bytes 131104 | tf_op jit(solution)/shard_map/ppermute | solution.py:177
  41.7 1.0 collective-permute-done.1.refs_1_
  42.7 1.6 %collective-permute-done.refs_0_ = bf16[128,512]{1,0:T(8,128)(2,1)S(1)} collective-permute-done((bf16[128,512]{1,0:T(8,128)(2,1)}, bf16[128,512]{1,0:T(8,128)(2,1)S(1)}, u32[]{:S(2)}, u32[]{:S(2)}) %collective-permute-start) | collective-permute-done | bytes 131104 | tf_op jit(solution)/shard_map/ppermute | solution.py:177
  44.3 3.3 %all-to-all-done = bf16[8,128,1536]{2,1,0:T(8,128)(2,1)S(1)} async-done(((bf16[8,128,1536]{2,1,0:T(8,128)(2,1)}), bf16[8,128,1536]{2,1,0:T(8,128)(2,1)S(1)}, u32[]{:S(2)}, u32[]{:S(2)}) %all-to-all-start) | async-done | bytes 3145760 | tf_op jit(solution)/shard_map/all_to_all | solution.py:18
  47.6 1.2 shard_map.60
  48.7 1.9 %collective-permute-start.4 = (bf16[4,4,32,512]{3,2,1,0:T(8,128)(2,1)S(1)}, bf16[4,4,32,512]{3,2,1,0:T(8,128)(2,1)S(1)}, u32[]{:S(2)}, u32[]{:S(2)}) collective-permute-start(bf16[4,4,32,512]{3,2,1,0:T(8,128)(2,1)S(1)} %shard_map.60), channel_id=1, source_target_pairs={{0,1},{1,0},{2,3},{3,2},{4,5},{5,4},{6,7},{7,6},{8,9},{9,8},{10,11... | collective-permute-start | bytes 1572872 | tf_op jit(solution)/shard_map/ppermute | solution.py:204
  50.7 1.0 pad_maximum_fusion.1
  51.7 0.0 copy-start.2
  51.7 0.9 pad_maximum_fusion.2
  52.6 2.4 %collective-permute-start.3 = (bf16[4,128,512]{2,1,0:T(8,128)(2,1)}, bf16[4,128,512]{2,1,0:T(8,128)(2,1)}, u32[]{:S(2)}, u32[]{:S(2)}) collective-permute-start(bf16[4,128,512]{2,1,0:T(8,128)(2,1)} %pad_maximum_fusion.2), channel_id=1, source_target_pairs={{0,1},{1,0},{2,3},{3,2},{4,5},{5,4},{6,7},{7,6},{8,9},{9,8},{10,11... | collective-permute-start | bytes 1572872 | tf_op jit(solution)/shard_map/ppermute | solution.py:187
  55.0 1.9 %shard_map.61 = bf16[4,4,32,512]{3,2,1,0:T(8,128)(2,1)} custom-call(s32[1]{0:T(128)} %bitcast.8.core_ref, bf16[1024,1536]{1,0:T(8,128)(2,1)S(1)} %bitcast.19, bf16[1024,1536]{1,0:T(8,128)(2,1)S(1)} %bitcast.20, bf16[4,4,32,512]{3,2,1,0:T(8,128)(2,1)S(1)} %collective-permute-done.4.refs_0_), custom_call_target="tpu_custom_call" | custom-call | flops 536870912 | bytes 3145728 | tf_op jit(solution)/shard_map/pallas_call | solution.py:71
  56.9 6.2 %all-to-all-start.1 = ((bf16[4,4,32,512]{3,2,1,0:T(8,128)(2,1)}), bf16[4,4,32,512]{3,2,1,0:T(8,128)(2,1)S(1)}, u32[]{:S(2)}, u32[]{:S(2)}) async-start(bf16[4,4,32,512]{3,2,1,0:T(8,128)(2,1)} %shard_map.61), calls=%async_computation.1 | async-start | bytes 1048576 | tf_op jit(solution)/shard_map/all_to_all | solution.py:18
  63.1 0.1 broadcast_bitcast_fusion
  63.2 1.2 select_bitcast_fusion.1
  64.4 0.1 pad_maximum_fusion
  64.5 0.1 copy.6
  64.7 1.0 copy-done.4
  65.7 1.4 convolution_convert_fusion.refs_0_
  67.0 0.0 copy-start.1
  67.1 12.5 %all-to-all-done.1.value_ref = bf16[4,4,32,512]{3,2,1,0:T(8,128)(2,1)S(1)} async-done(((bf16[4,4,32,512]{3,2,1,0:T(8,128)(2,1)}), bf16[4,4,32,512]{3,2,1,0:T(8,128)(2,1)S(1)}, u32[]{:S(2)}, u32[]{:S(2)}) %all-to-all-start.1) | async-done | bytes 524320 | tf_op jit(solution)/shard_map/all_to_all | solution.py:18
  79.5 0.1 shard_map.62
  79.6 26.8 %all_to_all.25.value_ref = bf16[12,48,128]{2,1,0:T(8,128)(2,1)S(1)} all-to-all(bf16[12,48,128]{2,1,0:T(8,128)(2,1)S(1)} %bitcast.22), channel_id=1, replica_groups=mesh['yh'=4,'yl'=2,'x'=4,'zl'=3,'zh'=4,'c'=2] {'zh','zl'}, dimensions={0} | all-to-all | bytes 294912 | tf_op jit(solution)/shard_map/all_to_all | solution.py:18
  106.5 13.9 %all_to_all.26 = bf16[12,48,128]{2,1,0:T(8,128)(2,1)S(1)} all-to-all(bf16[12,48,128]{2,1,0:T(8,128)(2,1)S(1)} %shard_map.63), channel_id=1, replica_groups=mesh['yh'=4,'yl'=2,'x'=4,'zl'=3,'zh'=4,'c'=2] {'yh','zl'}, dimensions={0} | all-to-all | bytes 294912 | tf_op jit(solution)/shard_map/all_to_all | solution.py:18
  120.4 0.2 shard_map.64
  120.6 17.4 %all_to_all.27 = bf16[8,4,32,512]{3,2,1,0:T(8,128)(2,1)S(1)} all-to-all(bf16[8,4,32,512]{3,2,1,0:T(8,128)(2,1)S(1)} %shard_map.64), channel_id=1, replica_groups=mesh['yh'=4,'yl'=2,'x'=4,'zl'=3,'zh'=4,'c'=2] {'x','yl'}, dimensions={0} | all-to-all | bytes 2097152 | tf_op jit(solution)/shard_map/all_to_all | solution.py:18
  138.0 1.6 %convert_multiply_fusion = f32[8,4,32,512]{3,2,1,0:T(8,128)} fusion(bf16[8,4,32,512]{3,2,1,0:T(8,128)(2,1)S(1)} %all_to_all.27), kind=kLoop, calls=%fused_computation | loop fusion | flops 1048576 | bytes 3145728 | tf_op jit(solution)/shard_map/mul | solution.py:216
  (10 shorter events, 0.1 us)
Async XLA Ops:
  0.6 62.5 %copy-start = (f32[8]{0:T(128)S(1)}, f32[8]{0:T(128)}, u32[]{:S(2)}) copy-start(f32[8]{0:T(128)} %param.7) | copy-start | bytes 100
  4.8 42.8 %all-to-all-start = ((bf16[8,128,1536]{2,1,0:T(8,128)(2,1)}), bf16[8,128,1536]{2,1,0:T(8,128)(2,1)S(1)}, u32[]{:S(2)}, u32[]{:S(2)}) async-start(bf16[8,128,1536]{2,1,0:T(8,128)(2,1)} %shard_map.59), calls=%async_computation | async-start | bytes 6291456 | tf_op jit(solution)/shard_map/all_to_all | solution.py:18
  17.8 23.9 %collective-permute-start.2 = (bf16[128,512]{1,0:T(8,128)(2,1)}, bf16[128,512]{1,0:T(8,128)(2,1)S(1)}, u32[]{:S(2)}, u32[]{:S(2)}) collective-permute-start(bf16[128,512]{1,0:T(8,128)(2,1)} %cot_ref.1), channel_id=1, source_target_pairs={{0,6},{2,0},{4,2},{6,4},{1,7},{3,1},{5,3},{7,5},{8,14},{10,8},{12,... | collective-permute-start | bytes 393224 | tf_op jit(solution)/shard_map/ppermute | solution.py:177
  25.1 17.6 %collective-permute-start.1 = (bf16[128,512]{1,0:T(8,128)(2,1)}, bf16[128,512]{1,0:T(8,128)(2,1)S(1)}, u32[]{:S(2)}, u32[]{:S(2)}) collective-permute-start(bf16[128,512]{1,0:T(8,128)(2,1)} %cot_ref.1), channel_id=1, source_target_pairs={{0,4},{2,6},{4,0},{6,2},{1,5},{3,7},{5,1},{7,3},{8,12},{10,14},{12... | collective-permute-start | bytes 393224 | tf_op jit(solution)/shard_map/ppermute | solution.py:177
  27.6 16.7 %collective-permute-start = (bf16[128,512]{1,0:T(8,128)(2,1)}, bf16[128,512]{1,0:T(8,128)(2,1)S(1)}, u32[]{:S(2)}, u32[]{:S(2)}) collective-permute-start(bf16[128,512]{1,0:T(8,128)(2,1)} %cot_ref.1), channel_id=1, source_target_pairs={{0,2},{2,4},{4,6},{6,0},{1,3},{3,5},{5,7},{7,1},{8,10},{10,12},{12... | collective-permute-start | bytes 393224 | tf_op jit(solution)/shard_map/ppermute | solution.py:177
  48.7 6.3 %collective-permute-start.4 = (bf16[4,4,32,512]{3,2,1,0:T(8,128)(2,1)S(1)}, bf16[4,4,32,512]{3,2,1,0:T(8,128)(2,1)S(1)}, u32[]{:S(2)}, u32[]{:S(2)}) collective-permute-start(bf16[4,4,32,512]{3,2,1,0:T(8,128)(2,1)S(1)} %shard_map.60), channel_id=1, source_target_pairs={{0,1},{1,0},{2,3},{3,2},{4,5},{5,4},{6,7},{7,6},{8,9},{9,8},{10,11... | collective-permute-start | bytes 1572872 | tf_op jit(solution)/shard_map/ppermute | solution.py:204
  51.7 0.9 copy-start.2
  51.7 3.3 %copy-start.3 = (bf16[1,128,512]{2,1,0:T(8,128)(2,1)}, bf16[1,128,512]{2,1,0:T(8,128)(2,1)S(1)}, u32[]{:S(2)}) copy-start(bf16[1,128,512]{2,1,0:T(8,128)(2,1)S(1)} %get-tuple-element.7) | copy-start | bytes 393220
  52.6 10.6 %collective-permute-start.3 = (bf16[4,128,512]{2,1,0:T(8,128)(2,1)}, bf16[4,128,512]{2,1,0:T(8,128)(2,1)}, u32[]{:S(2)}, u32[]{:S(2)}) collective-permute-start(bf16[4,128,512]{2,1,0:T(8,128)(2,1)} %pad_maximum_fusion.2), channel_id=1, source_target_pairs={{0,1},{1,0},{2,3},{3,2},{4,5},{5,4},{6,7},{7,6},{8,9},{9,8},{10,11... | collective-permute-start | bytes 1572872 | tf_op jit(solution)/shard_map/ppermute | solution.py:187
  56.9 22.6 %all-to-all-start.1 = ((bf16[4,4,32,512]{3,2,1,0:T(8,128)(2,1)}), bf16[4,4,32,512]{3,2,1,0:T(8,128)(2,1)S(1)}, u32[]{:S(2)}, u32[]{:S(2)}) async-start(bf16[4,4,32,512]{3,2,1,0:T(8,128)(2,1)} %shard_map.61), calls=%async_computation.1 | async-start | bytes 1048576 | tf_op jit(solution)/shard_map/all_to_all | solution.py:18
  64.4 1.2 copy-start.4
  67.0 53.5 %copy-start.1 = (bf16[1024,1024]{1,0:T(8,128)(2,1)}, bf16[1024,1024]{1,0:T(8,128)(2,1)S(1)}, u32[]{:S(2)}) copy-start(bf16[1024,1024]{1,0:T(8,128)(2,1)S(1)} %convolution_convert_fusion.refs_0_) | copy-start | bytes 6291460

commit v5 on v4

--- a/solution.py
+++ b/solution.py
@@ -178,12 +178,22 @@
     ]
 
 
-def gather_node(mine):
-    here = lax.axis_index("zh")
-    stack = jnp.stack(mine)
-    ordered = jnp.concatenate(
-        [lax.dynamic_slice_in_dim(stack, (here - j) % NZH, 1, 0) for j in range(NZH)], axis=0
-    )
+def in_order(mine):
+    def kernel(zh_ref, *refs):
+        for k in range(NZH):
+            refs[-1][lax.rem(zh_ref[0] + (NZH - k), NZH)] = refs[k][...]
+
+    return pl.pallas_call(
+        kernel,
+        in_specs=[pl.BlockSpec(memory_space=pltpu.SMEM)] + [pl.BlockSpec(memory_space=pltpu.VMEM)] * NZH,
+        out_specs=pl.BlockSpec(memory_space=pltpu.VMEM),
+        out_shape=jax.ShapeDtypeStruct((NZH,) + mine[0].shape, jnp.bfloat16),
+        compiler_params=SMALL,
+        cost_estimate=pl.CostEstimate(flops=0, bytes_accessed=4 * NZH * mine[0].size, transcendentals=0),
+    )(lax.axis_index("zh")[None], *mine)
+
+
+def gather_node(ordered):
     other = lax.ppermute(ordered, "c", [(0, 1), (1, 0)])
     first = lax.axis_index("c") == 0
     return jnp.stack([jnp.where(first, ordered, other), jnp.where(first, other, ordered)], axis=1)
@@ -199,12 +209,12 @@
 
     core = lax.axis_index("c")[None]
     got = exchange(lay_out(acts, cotangent), ("x", "yl")).reshape(NEAR * tok, NODE * part + head)
-    mine = gather_zh(cotangent)
-    theirs = product(got, head, 1 - core, after=mine[1:])
+    ordered = in_order(gather_zh(cotangent))
+    theirs = product(got, head, 1 - core, after=[ordered])
     chip = product(got, head, core, received=lax.ppermute(theirs, "c", [(0, 1), (1, 0)]))
 
     over_y = exchange(chip, "yh")
-    peers = gather_node(mine).reshape(NODE * tok, head)
+    peers = gather_node(ordered).reshape(NODE * tok, head)
     input_grad = input_gradient(peers, w_values, w_scales)
 
     slots = sum_y(over_y, [input_grad])

time: 140 us -> 138 us (0.986)
  other arithmetic: 4.81 us -> 2.99 us
  Pallas kernels: 7.48 us -> 9.18 us
    all_to_all x2, waiting for transfers between devices: 15.8 us -> 13 us  [exchange(): return lax.all_to_all(value, axes, split_axis=0, concat_axis=0, tiled=True)]
    ppermute x3, waiting for transfers between devices: 10.3 us -> 12.3 us  [gather_zh(): lax.ppermute(cotangent, 'zh', [(i, (i + k) % NZH) for i in range(NZH)])]
    pallas_call x0 -> x1, Pallas kernels: none -> 1.74 us  [in_order(): pl.pallas_call(kernel, in_specs=[pl.BlockSpec(memory_space=pltpu.SMEM)] +...]
  transfers between devices with their start and end apart: 7 -> 7, of which waited for: 5 -> 2; matrix products, arithmetic and copies ran while one was open for 3% -> 2% of each run, Pallas kernels for 1% -> 3%
where the time goes in v5:
time: 138 us
  blocking collectives  57.1 us (41%)
  starting transfers between devices  39.8 us (29%)
  waiting for transfers between devices  25.3 us (18%)
  Pallas kernels  9.18 us (7%)
  other arithmetic  2.99 us (2%)
    all_to_all x3, blocking collectives, exchange(): return lax.all_to_all(value, axes, split_axis=0, concat_axis=0, tiled=True)  57.1 us
    all_to_all x2, starting transfers between devices, exchange(): return lax.all_to_all(value, axes, split_axis=0, concat_axis=0, tiled=True)  19.3 us
    ppermute x3, starting transfers between devices, gather_zh(): lax.ppermute(cotangent, 'zh', [(i, (i + k) % NZH) for i in range(NZH)])  16.1 us
    all_to_all x2, waiting for transfers between devices, exchange(): return lax.all_to_all(value, axes, split_axis=0, concat_axis=0, tiled=True)  13 us
    ppermute x3, waiting for transfers between devices, gather_zh(): lax.ppermute(cotangent, 'zh', [(i, (i + k) % NZH) for i in range(NZH)])  12.3 us
    pallas_call x1, Pallas kernels, lay_out(): pl.pallas_call(kernel, grid=(tok // step,), in_specs=[pl.BlockSpec((step,...  4.13 us
    pallas_call x2, Pallas kernels, product(): pl.pallas_call(kernel, grid_spec=pltpu.PrefetchScalarGridSpec(num_scalar_...  3.06 us
  transfers between devices with their start and end apart: 7, of which 2 were waited for; matrix products, arithmetic and copies ran while one was open for 2% of the time, Pallas kernels for 3%

profile of v5, /device:TPU:8, one launch (start us, length us, event | category | flops | bytes accessed | tf_op | source)
XLA Modules:
  0.0 137.8 jit_solution(3660541076887258595)
XLA Ops:
  0.6 0.0 copy-start
  0.6 4.1 %shard_map.60 = bf16[8,128,1536]{2,1,0:T(8,128)(2,1)} custom-call(bf16[128,8192]{1,0:T(8,128)(2,1)} %acts_ref.1, bf16[128,512]{1,0:T(8,128)(2,1)} %cot_ref.1), custom_call_target="tpu_custom_call" | custom-call | bytes 6291456 | tf_op jit(solution)/shard_map/pallas_call | solution.py:36
  4.8 13.1 %all-to-all-start = ((bf16[8,128,1536]{2,1,0:T(8,128)(2,1)}), bf16[8,128,1536]{2,1,0:T(8,128)(2,1)S(1)}, u32[]{:S(2)}, u32[]{:S(2)}) async-start(bf16[8,128,1536]{2,1,0:T(8,128)(2,1)} %shard_map.60), calls=%async_computation | async-start | bytes 6291456 | tf_op jit(solution)/shard_map/all_to_all | solution.py:18
  17.9 1.9 %collective-permute-start = (bf16[128,512]{1,0:T(8,128)(2,1)S(1)}, bf16[128,512]{1,0:T(8,128)(2,1)S(1)}, u32[]{:S(2)}, u32[]{:S(2)}) collective-permute-start(bf16[128,512]{1,0:T(8,128)(2,1)S(1)} %copy-done.2), channel_id=1, source_target_pairs={{0,2},{2,4},{4,6},{6,0},{1,3},{3,5},{5,7},{7,1},{8,10},{10,12},{12... | collective-permute-start | bytes 393224 | tf_op jit(solution)/shard_map/ppermute | solution.py:177
  19.8 11.8 %collective-permute-start.1 = (bf16[128,512]{1,0:T(8,128)(2,1)S(1)}, bf16[128,512]{1,0:T(8,128)(2,1)S(1)}, u32[]{:S(2)}, u32[]{:S(2)}) collective-permute-start(bf16[128,512]{1,0:T(8,128)(2,1)S(1)} %copy-done.2), channel_id=1, source_target_pairs={{0,4},{2,6},{4,0},{6,2},{1,5},{3,7},{5,1},{7,3},{8,12},{10,14},{12... | collective-permute-start | bytes 393224 | tf_op jit(solution)/shard_map/ppermute | solution.py:177
  31.6 2.4 %collective-permute-start.2 = (bf16[128,512]{1,0:T(8,128)(2,1)S(1)}, bf16[128,512]{1,0:T(8,128)(2,1)}, u32[]{:S(2)}, u32[]{:S(2)}) collective-permute-start(bf16[128,512]{1,0:T(8,128)(2,1)S(1)} %copy-done.2), channel_id=1, source_target_pairs={{0,6},{2,0},{4,2},{6,4},{1,7},{3,1},{5,3},{7,5},{8,14},{10,8},{12,... | collective-permute-start | bytes 393224 | tf_op jit(solution)/shard_map/ppermute | solution.py:177
  34.1 0.0 collective-permute-done.refs_1_
  34.1 12.3 %collective-permute-done.1.refs_2_ = bf16[128,512]{1,0:T(8,128)(2,1)S(1)} collective-permute-done((bf16[128,512]{1,0:T(8,128)(2,1)S(1)}, bf16[128,512]{1,0:T(8,128)(2,1)S(1)}, u32[]{:S(2)}, u32[]{:S(2)}) %collective-permute-start.1) | collective-permute-done | bytes 131104 | tf_op jit(solution)/shard_map/ppermute | solution.py:177
  46.3 0.0 collective-permute-done.2.refs_3_
  46.4 1.7 %shard_map.59.refs_0_ = bf16[4,128,512]{2,1,0:T(8,128)(2,1)} custom-call(s32[1]{0:T(128)} %bitcast.zh_ref, bf16[128,512]{1,0:T(8,128)(2,1)S(1)} %copy-done.2, bf16[128,512]{1,0:T(8,128)(2,1)S(1)} %collective-permute-done.refs_1_, bf16[128,512]{1,0:T(8,128)(2,1)S(1)} %collective-permute-done.1.refs_2_, bf16[128,512]{1,0:T(8,128)(2,1)} %collective-permute-done.2.refs_3_), custom_call_target="tpu_custom_call" | custom-call | bytes 1048576 | tf_op jit(solution)/shard_map/pallas_call | solution.py:186
  48.1 0.0 all-to-all-done
  48.1 1.2 shard_map.61
  49.3 1.9 %collective-permute-start.4 = (bf16[4,4,32,512]{3,2,1,0:T(8,128)(2,1)S(1)}, bf16[4,4,32,512]{3,2,1,0:T(8,128)(2,1)S(1)}, u32[]{:S(2)}, u32[]{:S(2)}) collective-permute-start(bf16[4,4,32,512]{3,2,1,0:T(8,128)(2,1)S(1)} %shard_map.61), channel_id=1, source_target_pairs={{0,1},{1,0},{2,3},{3,2},{4,5},{5,4},{6,7},{7,6},{8,9},{9,8},{10,11... | collective-permute-start | bytes 1572872 | tf_op jit(solution)/shard_map/ppermute | solution.py:214
  51.2 2.4 %collective-permute-start.3 = (bf16[4,128,512]{2,1,0:T(8,128)(2,1)}, bf16[4,128,512]{2,1,0:T(8,128)(2,1)}, u32[]{:S(2)}, u32[]{:S(2)}) collective-permute-start(bf16[4,128,512]{2,1,0:T(8,128)(2,1)} %shard_map.59.refs_0_), channel_id=1, source_target_pairs={{0,1},{1,0},{2,3},{3,2},{4,5},{5,4},{6,7},{7,6},{8,9},{9,8},{10,11... | collective-permute-start | bytes 1572872 | tf_op jit(solution)/shard_map/ppermute | solution.py:197
  53.6 0.0 collective-permute-done.4.refs_0_
  53.6 1.9 %shard_map.62 = bf16[4,4,32,512]{3,2,1,0:T(8,128)(2,1)} custom-call(s32[1]{0:T(128)} %bitcast.5.core_ref, bf16[1024,1536]{1,0:T(8,128)(2,1)S(1)} %bitcast.16, bf16[1024,1536]{1,0:T(8,128)(2,1)S(1)} %bitcast.17, bf16[4,4,32,512]{3,2,1,0:T(8,128)(2,1)S(1)} %collective-permute-done.4.refs_0_), custom_call_target="tpu_custom_call" | custom-call | flops 536870912 | bytes 3145728 | tf_op jit(solution)/shard_map/pallas_call | solution.py:71
  55.5 6.2 %all-to-all-start.1 = ((bf16[4,4,32,512]{3,2,1,0:T(8,128)(2,1)}), bf16[4,4,32,512]{3,2,1,0:T(8,128)(2,1)S(1)}, u32[]{:S(2)}, u32[]{:S(2)}) async-start(bf16[4,4,32,512]{3,2,1,0:T(8,128)(2,1)} %shard_map.62), calls=%async_computation.1 | async-start | bytes 1048576 | tf_op jit(solution)/shard_map/all_to_all | solution.py:18
  61.7 0.1 broadcast_bitcast_fusion
  61.8 1.3 select_bitcast_fusion.1
  63.1 0.0 copy-start.3
  63.1 0.1 pad_maximum_fusion
  63.2 0.1 copy.6
  63.3 1.0 copy-done.3
  64.3 1.4 %convolution_convert_fusion.refs_0_ = bf16[1024,1024]{1,0:T(8,128)(2,1)S(1)} fusion(bf16[1024,512]{1,0:T(8,128)(2,1)S(1)} %bitcast.21, bf16[1024,512]{1,0:T(8,128)(2,1)S(1)} %copy-done.3, f32[1024]{0:T(1024)S(1)} %broadcast_bitcast_fusion), kind=kOutput, calls=%fused_computation.2 | convolution fusion | flops 1076363264 | bytes 4198400 | tf_op jit(solution)/shard_map/dot_general | solution.py:169
  65.7 0.0 copy-start.1
  65.7 13.0 %all-to-all-done.1.value_ref = bf16[4,4,32,512]{3,2,1,0:T(8,128)(2,1)S(1)} async-done(((bf16[4,4,32,512]{3,2,1,0:T(8,128)(2,1)}), bf16[4,4,32,512]{3,2,1,0:T(8,128)(2,1)S(1)}, u32[]{:S(2)}, u32[]{:S(2)}) %all-to-all-start.1) | async-done | bytes 524320 | tf_op jit(solution)/shard_map/all_to_all | solution.py:18
  78.7 0.1 shard_map.63
  78.8 25.8 %all_to_all.25.value_ref = bf16[12,48,128]{2,1,0:T(8,128)(2,1)S(1)} all-to-all(bf16[12,48,128]{2,1,0:T(8,128)(2,1)S(1)} %bitcast.19), channel_id=1, replica_groups=mesh['yh'=4,'yl'=2,'x'=4,'zl'=3,'zh'=4,'c'=2] {'zh','zl'}, dimensions={0} | all-to-all | bytes 294912 | tf_op jit(solution)/shard_map/all_to_all | solution.py:18
  104.6 13.9 %all_to_all.26 = bf16[12,48,128]{2,1,0:T(8,128)(2,1)S(1)} all-to-all(bf16[12,48,128]{2,1,0:T(8,128)(2,1)S(1)} %shard_map.64), channel_id=1, replica_groups=mesh['yh'=4,'yl'=2,'x'=4,'zl'=3,'zh'=4,'c'=2] {'yh','zl'}, dimensions={0} | all-to-all | bytes 294912 | tf_op jit(solution)/shard_map/all_to_all | solution.py:18
  118.5 0.2 shard_map.65
  118.7 17.4 %all_to_all.27 = bf16[8,4,32,512]{3,2,1,0:T(8,128)(2,1)S(1)} all-to-all(bf16[8,4,32,512]{3,2,1,0:T(8,128)(2,1)S(1)} %shard_map.65), channel_id=1, replica_groups=mesh['yh'=4,'yl'=2,'x'=4,'zl'=3,'zh'=4,'c'=2] {'x','yl'}, dimensions={0} | all-to-all | bytes 2097152 | tf_op jit(solution)/shard_map/all_to_all | solution.py:18
  136.1 1.6 %convert_multiply_fusion = f32[8,4,32,512]{3,2,1,0:T(8,128)} fusion(bf16[8,4,32,512]{3,2,1,0:T(8,128)(2,1)S(1)} %all_to_all.27), kind=kLoop, calls=%fused_computation | loop fusion | flops 1048576 | bytes 3145728 | tf_op jit(solution)/shard_map/mul | solution.py:226
  (6 shorter events, 0.0 us)
Async XLA Ops:
  0.6 61.1 %copy-start = (f32[8]{0:T(128)S(1)}, f32[8]{0:T(128)}, u32[]{:S(2)}) copy-start(f32[8]{0:T(128)} %param.7) | copy-start | bytes 100
  4.8 13.1 %copy-start.2 = (bf16[128,512]{1,0:T(8,128)(2,1)S(1)}, bf16[128,512]{1,0:T(8,128)(2,1)}, u32[]{:S(2)}) copy-start(bf16[128,512]{1,0:T(8,128)(2,1)} %cot_ref.1) | copy-start | bytes 393220
  4.8 43.3 %all-to-all-start = ((bf16[8,128,1536]{2,1,0:T(8,128)(2,1)}), bf16[8,128,1536]{2,1,0:T(8,128)(2,1)S(1)}, u32[]{:S(2)}, u32[]{:S(2)}) async-start(bf16[8,128,1536]{2,1,0:T(8,128)(2,1)} %shard_map.60), calls=%async_computation | async-start | bytes 6291456 | tf_op jit(solution)/shard_map/all_to_all | solution.py:18
  17.9 16.2 %collective-permute-start = (bf16[128,512]{1,0:T(8,128)(2,1)S(1)}, bf16[128,512]{1,0:T(8,128)(2,1)S(1)}, u32[]{:S(2)}, u32[]{:S(2)}) collective-permute-start(bf16[128,512]{1,0:T(8,128)(2,1)S(1)} %copy-done.2), channel_id=1, source_target_pairs={{0,2},{2,4},{4,6},{6,0},{1,3},{3,5},{5,7},{7,1},{8,10},{10,12},{12... | collective-permute-start | bytes 393224 | tf_op jit(solution)/shard_map/ppermute | solution.py:177
  19.8 26.5 %collective-permute-start.1 = (bf16[128,512]{1,0:T(8,128)(2,1)S(1)}, bf16[128,512]{1,0:T(8,128)(2,1)S(1)}, u32[]{:S(2)}, u32[]{:S(2)}) collective-permute-start(bf16[128,512]{1,0:T(8,128)(2,1)S(1)} %copy-done.2), channel_id=1, source_target_pairs={{0,4},{2,6},{4,0},{6,2},{1,5},{3,7},{5,1},{7,3},{8,12},{10,14},{12... | collective-permute-start | bytes 393224 | tf_op jit(solution)/shard_map/ppermute | solution.py:177
  31.6 14.7 %collective-permute-start.2 = (bf16[128,512]{1,0:T(8,128)(2,1)S(1)}, bf16[128,512]{1,0:T(8,128)(2,1)}, u32[]{:S(2)}, u32[]{:S(2)}) collective-permute-start(bf16[128,512]{1,0:T(8,128)(2,1)S(1)} %copy-done.2), channel_id=1, source_target_pairs={{0,6},{2,0},{4,2},{6,4},{1,7},{3,1},{5,3},{7,5},{8,14},{10,8},{12,... | collective-permute-start | bytes 393224 | tf_op jit(solution)/shard_map/ppermute | solution.py:177
  49.3 4.3 %collective-permute-start.4 = (bf16[4,4,32,512]{3,2,1,0:T(8,128)(2,1)S(1)}, bf16[4,4,32,512]{3,2,1,0:T(8,128)(2,1)S(1)}, u32[]{:S(2)}, u32[]{:S(2)}) collective-permute-start(bf16[4,4,32,512]{3,2,1,0:T(8,128)(2,1)S(1)} %shard_map.61), channel_id=1, source_target_pairs={{0,1},{1,0},{2,3},{3,2},{4,5},{5,4},{6,7},{7,6},{8,9},{9,8},{10,11... | collective-permute-start | bytes 1572872 | tf_op jit(solution)/shard_map/ppermute | solution.py:214
  51.2 10.6 %collective-permute-start.3 = (bf16[4,128,512]{2,1,0:T(8,128)(2,1)}, bf16[4,128,512]{2,1,0:T(8,128)(2,1)}, u32[]{:S(2)}, u32[]{:S(2)}) collective-permute-start(bf16[4,128,512]{2,1,0:T(8,128)(2,1)} %shard_map.59.refs_0_), channel_id=1, source_target_pairs={{0,1},{1,0},{2,3},{3,2},{4,5},{5,4},{6,7},{7,6},{8,9},{9,8},{10,11... | collective-permute-start | bytes 1572872 | tf_op jit(solution)/shard_map/ppermute | solution.py:197
  55.5 23.2 %all-to-all-start.1 = ((bf16[4,4,32,512]{3,2,1,0:T(8,128)(2,1)}), bf16[4,4,32,512]{3,2,1,0:T(8,128)(2,1)S(1)}, u32[]{:S(2)}, u32[]{:S(2)}) async-start(bf16[4,4,32,512]{3,2,1,0:T(8,128)(2,1)} %shard_map.62), calls=%async_computation.1 | async-start | bytes 1048576 | tf_op jit(solution)/shard_map/all_to_all | solution.py:18
  63.1 1.2 copy-start.3
  65.7 53.0 %copy-start.1 = (bf16[1024,1024]{1,0:T(8,128)(2,1)}, bf16[1024,1024]{1,0:T(8,128)(2,1)S(1)}, u32[]{:S(2)}) copy-start(bf16[1024,1024]{1,0:T(8,128)(2,1)S(1)} %convolution_convert_fusion.refs_0_) | copy-start | bytes 6291460

commit v6 on v5

--- a/solution.py
+++ b/solution.py
@@ -22,26 +22,49 @@
     tok, width = acts.shape
     head = cotangent.shape[1]
     part = width // (NODE * NEAR)
-    step = 32
-
-    def kernel(acts_ref, cot_ref, out_ref):
-        for s in range(NEAR):
-            for c in range(NC):
-                for zh in range(NZH):
-                    to, source = (c * NZH + zh) * part, ((zh * NC + c) * NEAR + s) * part
-                    out_ref[s, :, to : to + part] = acts_ref[:, source : source + part]
-            out_ref[s, :, NODE * part :] = cot_ref[...]
-
+    step = 16
+    chunks = tok // step
     out = (NEAR, tok, NODE * part + head)
-    return pl.pallas_call(
-        kernel,
-        grid=(tok // step,),
-        in_specs=[
-            pl.BlockSpec((step, width), lambda i: (i, 0)),
-            pl.BlockSpec((step, head), lambda i: (i, 0)),
+
+    def kernel(acts_ref, cot_ref, out_ref, acts_in, cot_in, laid, acts_sem, cot_sem, out_sem):
+        def rows(i):
+            return pl.ds(i * step, step)
+
+        cot_copy = pltpu.make_async_copy(cot_ref, cot_in, cot_sem)
+        cot_copy.start()
+        reads = [
+            pltpu.make_async_copy(acts_ref.at[rows(i)], acts_in.at[rows(i)], acts_sem.at[i]) for i in range(chunks)
+        ]
+        for read in reads:
+            read.start()
+        cot_copy.wait()
+        writes = []
+        for i in range(chunks):
+            reads[i].wait()
+            for s in range(NEAR):
+                for c in range(NC):
+                    for zh in range(NZH):
+                        to, source = (c * NZH + zh) * part, ((zh * NC + c) * NEAR + s) * part
+                        laid[s, rows(i), to : to + part] = acts_in[rows(i), source : source + part]
+                laid[s, rows(i), NODE * part :] = cot_in[rows(i), :]
+            writes.append(pltpu.make_async_copy(laid.at[:, rows(i)], out_ref.at[:, rows(i)], out_sem.at[i]))
+            writes[-1].start()
+        for write in writes:
+            write.wait()
+
+    return pl.pallas_call(
+        kernel,
+        in_specs=[pl.BlockSpec(memory_space=pl.ANY)] * 2,
+        out_specs=pl.BlockSpec(memory_space=pl.ANY),
+        out_shape=pltpu.HBM(out, jnp.bfloat16),
+        scratch_shapes=[
+            pltpu.VMEM((tok, width), jnp.bfloat16),
+            pltpu.VMEM((tok, head), jnp.bfloat16),
+            pltpu.VMEM(out, jnp.bfloat16),
+            pltpu.SemaphoreType.DMA((chunks,)),
+            pltpu.SemaphoreType.DMA,
+            pltpu.SemaphoreType.DMA((chunks,)),
         ],
-        out_specs=pl.BlockSpec((NEAR, step, out[2]), lambda i: (0, i, 0)),
-        out_shape=pltpu.HBM(out, jnp.bfloat16),
         compiler_params=LARGE,
         cost_estimate=pl.CostEstimate(flops=0, bytes_accessed=4 * NEAR * tok * out[2], transcendentals=0),
     )(acts, cotangent)
@@ -208,7 +231,7 @@
     factor = (tok * NYH * NYL * NX * NZL * NZH * NC) ** (-0.5)
 
     core = lax.axis_index("c")[None]
-    got = exchange(lay_out(acts, cotangent), ("x", "yl")).reshape(NEAR * tok, NODE * part + head)
+    got = exchange(lay_out(acts, cotangent), ("yl", "x")).reshape(NEAR * tok, NODE * part + head)
     ordered = in_order(gather_zh(cotangent))
     theirs = product(got, head, 1 - core, after=[ordered])
     chip = product(got, head, core, received=lax.ppermute(theirs, "c", [(0, 1), (1, 0)]))
@@ -222,7 +245,7 @@
     copies = sum_z(exchange(slots, ("zh", "zl")))
     back = exchange(copies, ("yh", "zl"))
     back = join(back.reshape((NYH, NZL) + back.shape[1:]), rows, head)
-    full = exchange(back, ("x", "yl")).reshape(owned, head)
+    full = exchange(back, ("yl", "x")).reshape(owned, head)
     return (input_grad, full.astype(jnp.float32) * factor)
 
 

time: 138 us -> 137 us (level)
  no operation moved by 1% of the time
where the time goes in v6:
time: 137 us; the launch traced here: 136 us
  blocking collectives  56.8 us (41%)
  starting transfers between devices  39.8 us (29%)
  waiting for transfers between devices  24.9 us (18%)
  Pallas kernels  8.35 us (6%)
  other arithmetic  2.99 us (2%)
  matrix products  1.38 us (1%)
    all_to_all x3, blocking collectives, exchange(): return lax.all_to_all(value, axes, split_axis=0, concat_axis=0, tiled=True)  56.8 us
    all_to_all x2, starting transfers between devices, exchange(): return lax.all_to_all(value, axes, split_axis=0, concat_axis=0, tiled=True)  19.4 us
    ppermute x3, starting transfers between devices, gather_zh(): lax.ppermute(cotangent, 'zh', [(i, (i + k) % NZH) for i in range(NZH)])  16.1 us
    all_to_all x2, waiting for transfers between devices, exchange(): return lax.all_to_all(value, axes, split_axis=0, concat_axis=0, tiled=True)  12.6 us
    ppermute x3, waiting for transfers between devices, gather_zh(): lax.ppermute(cotangent, 'zh', [(i, (i + k) % NZH) for i in range(NZH)])  12.3 us
    pallas_call x1, Pallas kernels, lay_out(): pl.pallas_call(kernel, in_specs=[pl.BlockSpec(memory_space=pl.ANY)] * 2,...  3.3 us
    pallas_call x2, Pallas kernels, product(): pl.pallas_call(kernel, grid_spec=pltpu.PrefetchScalarGridSpec(num_scalar_...  3.06 us
  transfers between devices with their start and end apart: 7, of which 2 were waited for; matrix products, arithmetic and copies ran while one was open for 2% of the time, Pallas kernels for 3%

profile of v6, /device:TPU:8, one launch (start us, length us, event | category | flops | bytes accessed | tf_op | source)
XLA Modules:
  0.0 136.2 jit_solution(13572982584582838740)
XLA Ops:
  0.6 0.0 copy-start
  0.6 3.3 %shard_map.60 = bf16[8,128,1536]{2,1,0:T(8,128)(2,1)} custom-call(bf16[128,8192]{1,0:T(8,128)(2,1)} %acts_ref.1, bf16[128,512]{1,0:T(8,128)(2,1)} %cot_ref.1), custom_call_target="tpu_custom_call" | custom-call | bytes 6291456 | tf_op jit(solution)/shard_map/pallas_call | solution.py:55
  3.9 0.0 copy-start.2
  4.0 13.2 %all-to-all-start = ((bf16[8,128,1536]{2,1,0:T(8,128)(2,1)}), bf16[8,128,1536]{2,1,0:T(8,128)(2,1)S(1)}, u32[]{:S(2)}, u32[]{:S(2)}) async-start(bf16[8,128,1536]{2,1,0:T(8,128)(2,1)} %shard_map.60), calls=%async_computation | async-start | bytes 6291456 | tf_op jit(solution)/shard_map/all_to_all | solution.py:18
  17.1 1.9 %collective-permute-start = (bf16[128,512]{1,0:T(8,128)(2,1)S(1)}, bf16[128,512]{1,0:T(8,128)(2,1)S(1)}, u32[]{:S(2)}, u32[]{:S(2)}) collective-permute-start(bf16[128,512]{1,0:T(8,128)(2,1)S(1)} %copy-done.2), channel_id=1, source_target_pairs={{0,2},{2,4},{4,6},{6,0},{1,3},{3,5},{5,7},{7,1},{8,10},{10,12},{12... | collective-permute-start | bytes 393224 | tf_op jit(solution)/shard_map/ppermute | solution.py:200
  19.1 11.8 %collective-permute-start.1 = (bf16[128,512]{1,0:T(8,128)(2,1)S(1)}, bf16[128,512]{1,0:T(8,128)(2,1)S(1)}, u32[]{:S(2)}, u32[]{:S(2)}) collective-permute-start(bf16[128,512]{1,0:T(8,128)(2,1)S(1)} %copy-done.2), channel_id=1, source_target_pairs={{0,4},{2,6},{4,0},{6,2},{1,5},{3,7},{5,1},{7,3},{8,12},{10,14},{12... | collective-permute-start | bytes 393224 | tf_op jit(solution)/shard_map/ppermute | solution.py:200
  30.8 2.4 %collective-permute-start.2 = (bf16[128,512]{1,0:T(8,128)(2,1)S(1)}, bf16[128,512]{1,0:T(8,128)(2,1)}, u32[]{:S(2)}, u32[]{:S(2)}) collective-permute-start(bf16[128,512]{1,0:T(8,128)(2,1)S(1)} %copy-done.2), channel_id=1, source_target_pairs={{0,6},{2,0},{4,2},{6,4},{1,7},{3,1},{5,3},{7,5},{8,14},{10,8},{12,... | collective-permute-start | bytes 393224 | tf_op jit(solution)/shard_map/ppermute | solution.py:200
  33.3 0.0 collective-permute-done.refs_1_
  33.3 12.3 %collective-permute-done.1.refs_2_ = bf16[128,512]{1,0:T(8,128)(2,1)S(1)} collective-permute-done((bf16[128,512]{1,0:T(8,128)(2,1)S(1)}, bf16[128,512]{1,0:T(8,128)(2,1)S(1)}, u32[]{:S(2)}, u32[]{:S(2)}) %collective-permute-start.1) | collective-permute-done | bytes 131104 | tf_op jit(solution)/shard_map/ppermute | solution.py:200
  45.6 0.0 collective-permute-done.2.refs_3_
  45.6 1.7 %shard_map.59.refs_0_ = bf16[4,128,512]{2,1,0:T(8,128)(2,1)} custom-call(s32[1]{0:T(128)} %bitcast.zh_ref, bf16[128,512]{1,0:T(8,128)(2,1)S(1)} %copy-done.2, bf16[128,512]{1,0:T(8,128)(2,1)S(1)} %collective-permute-done.refs_1_, bf16[128,512]{1,0:T(8,128)(2,1)S(1)} %collective-permute-done.1.refs_2_, bf16[128,512]{1,0:T(8,128)(2,1)} %collective-permute-done.2.refs_3_), custom_call_target="tpu_custom_call" | custom-call | bytes 1048576 | tf_op jit(solution)/shard_map/pallas_call | solution.py:209
  47.3 1.2 shard_map.61
  48.5 1.9 %collective-permute-start.4 = (bf16[4,4,32,512]{3,2,1,0:T(8,128)(2,1)S(1)}, bf16[4,4,32,512]{3,2,1,0:T(8,128)(2,1)S(1)}, u32[]{:S(2)}, u32[]{:S(2)}) collective-permute-start(bf16[4,4,32,512]{3,2,1,0:T(8,128)(2,1)S(1)} %shard_map.61), channel_id=1, source_target_pairs={{0,1},{1,0},{2,3},{3,2},{4,5},{5,4},{6,7},{7,6},{8,9},{9,8},{10,11... | collective-permute-start | bytes 1572872 | tf_op jit(solution)/shard_map/ppermute | solution.py:237
  50.4 2.4 %collective-permute-start.3 = (bf16[4,128,512]{2,1,0:T(8,128)(2,1)}, bf16[4,128,512]{2,1,0:T(8,128)(2,1)}, u32[]{:S(2)}, u32[]{:S(2)}) collective-permute-start(bf16[4,128,512]{2,1,0:T(8,128)(2,1)} %shard_map.59.refs_0_), channel_id=1, source_target_pairs={{0,1},{1,0},{2,3},{3,2},{4,5},{5,4},{6,7},{7,6},{8,9},{9,8},{10,11... | collective-permute-start | bytes 1572872 | tf_op jit(solution)/shard_map/ppermute | solution.py:220
  52.8 0.0 collective-permute-done.4.refs_0_
  52.8 1.9 %shard_map.62 = bf16[4,4,32,512]{3,2,1,0:T(8,128)(2,1)} custom-call(s32[1]{0:T(128)} %bitcast.5.core_ref, bf16[1024,1536]{1,0:T(8,128)(2,1)S(1)} %bitcast.16, bf16[1024,1536]{1,0:T(8,128)(2,1)S(1)} %bitcast.17, bf16[4,4,32,512]{3,2,1,0:T(8,128)(2,1)S(1)} %collective-permute-done.4.refs_0_), custom_call_target="tpu_custom_call" | custom-call | flops 536870912 | bytes 3145728 | tf_op jit(solution)/shard_map/pallas_call | solution.py:94
  54.7 6.2 %all-to-all-start.1 = ((bf16[4,4,32,512]{3,2,1,0:T(8,128)(2,1)}), bf16[4,4,32,512]{3,2,1,0:T(8,128)(2,1)S(1)}, u32[]{:S(2)}, u32[]{:S(2)}) async-start(bf16[4,4,32,512]{3,2,1,0:T(8,128)(2,1)} %shard_map.62), calls=%async_computation.1 | async-start | bytes 1048576 | tf_op jit(solution)/shard_map/all_to_all | solution.py:18
  60.9 0.1 broadcast_bitcast_fusion
  61.0 1.3 select_bitcast_fusion.1
  62.3 0.0 copy-start.3
  62.3 0.1 pad_maximum_fusion
  62.4 0.1 copy.6
  62.5 1.0 copy-done.3
  63.5 1.4 %convolution_convert_fusion.refs_0_ = bf16[1024,1024]{1,0:T(8,128)(2,1)S(1)} fusion(bf16[1024,512]{1,0:T(8,128)(2,1)S(1)} %bitcast.21, bf16[1024,512]{1,0:T(8,128)(2,1)S(1)} %copy-done.3, f32[1024]{0:T(1024)S(1)} %broadcast_bitcast_fusion), kind=kOutput, calls=%fused_computation.2 | convolution fusion | flops 1076363264 | bytes 4198400 | tf_op jit(solution)/shard_map/dot_general | solution.py:192
  64.9 0.0 copy-start.1
  64.9 12.6 %all-to-all-done.1.value_ref = bf16[4,4,32,512]{3,2,1,0:T(8,128)(2,1)S(1)} async-done(((bf16[4,4,32,512]{3,2,1,0:T(8,128)(2,1)}), bf16[4,4,32,512]{3,2,1,0:T(8,128)(2,1)S(1)}, u32[]{:S(2)}, u32[]{:S(2)}) %all-to-all-start.1) | async-done | bytes 524320 | tf_op jit(solution)/shard_map/all_to_all | solution.py:18
  77.5 0.1 shard_map.63
  77.5 26.3 %all_to_all.25.value_ref = bf16[12,48,128]{2,1,0:T(8,128)(2,1)S(1)} all-to-all(bf16[12,48,128]{2,1,0:T(8,128)(2,1)S(1)} %bitcast.19), channel_id=1, replica_groups=mesh['yh'=4,'yl'=2,'x'=4,'zl'=3,'zh'=4,'c'=2] {'zh','zl'}, dimensions={0} | all-to-all | bytes 294912 | tf_op jit(solution)/shard_map/all_to_all | solution.py:18
  103.9 14.2 %all_to_all.26 = bf16[12,48,128]{2,1,0:T(8,128)(2,1)S(1)} all-to-all(bf16[12,48,128]{2,1,0:T(8,128)(2,1)S(1)} %shard_map.64), channel_id=1, replica_groups=mesh['yh'=4,'yl'=2,'x'=4,'zl'=3,'zh'=4,'c'=2] {'yh','zl'}, dimensions={0} | all-to-all | bytes 294912 | tf_op jit(solution)/shard_map/all_to_all | solution.py:18
  118.1 0.2 shard_map.65
  118.3 16.3 %all_to_all.27 = bf16[8,4,32,512]{3,2,1,0:T(8,128)(2,1)S(1)} all-to-all(bf16[8,4,32,512]{3,2,1,0:T(8,128)(2,1)S(1)} %shard_map.65), channel_id=1, replica_groups=mesh['yh'=4,'yl'=2,'x'=4,'zl'=3,'zh'=4,'c'=2] {'yl','x'}, dimensions={0} | all-to-all | bytes 2097152 | tf_op jit(solution)/shard_map/all_to_all | solution.py:18
  134.5 1.6 %convert_multiply_fusion = f32[8,4,32,512]{3,2,1,0:T(8,128)} fusion(bf16[8,4,32,512]{3,2,1,0:T(8,128)(2,1)S(1)} %all_to_all.27), kind=kLoop, calls=%fused_computation | loop fusion | flops 1048576 | bytes 3145728 | tf_op jit(solution)/shard_map/mul | solution.py:249
  (6 shorter events, 0.0 us)
Async XLA Ops:
  0.6 60.3 %copy-start = (f32[8]{0:T(128)S(1)}, f32[8]{0:T(128)}, u32[]{:S(2)}) copy-start(f32[8]{0:T(128)} %param.7) | copy-start | bytes 100
  3.9 13.2 %copy-start.2 = (bf16[128,512]{1,0:T(8,128)(2,1)S(1)}, bf16[128,512]{1,0:T(8,128)(2,1)}, u32[]{:S(2)}) copy-start(bf16[128,512]{1,0:T(8,128)(2,1)} %cot_ref.1) | copy-start | bytes 393220
  4.0 43.3 %all-to-all-start = ((bf16[8,128,1536]{2,1,0:T(8,128)(2,1)}), bf16[8,128,1536]{2,1,0:T(8,128)(2,1)S(1)}, u32[]{:S(2)}, u32[]{:S(2)}) async-start(bf16[8,128,1536]{2,1,0:T(8,128)(2,1)} %shard_map.60), calls=%async_computation | async-start | bytes 6291456 | tf_op jit(solution)/shard_map/all_to_all | solution.py:18
  17.1 16.1 %collective-permute-start = (bf16[128,512]{1,0:T(8,128)(2,1)S(1)}, bf16[128,512]{1,0:T(8,128)(2,1)S(1)}, u32[]{:S(2)}, u32[]{:S(2)}) collective-permute-start(bf16[128,512]{1,0:T(8,128)(2,1)S(1)} %copy-done.2), channel_id=1, source_target_pairs={{0,2},{2,4},{4,6},{6,0},{1,3},{3,5},{5,7},{7,1},{8,10},{10,12},{12... | collective-permute-start | bytes 393224 | tf_op jit(solution)/shard_map/ppermute | solution.py:200
  19.1 26.5 %collective-permute-start.1 = (bf16[128,512]{1,0:T(8,128)(2,1)S(1)}, bf16[128,512]{1,0:T(8,128)(2,1)S(1)}, u32[]{:S(2)}, u32[]{:S(2)}) collective-permute-start(bf16[128,512]{1,0:T(8,128)(2,1)S(1)} %copy-done.2), channel_id=1, source_target_pairs={{0,4},{2,6},{4,0},{6,2},{1,5},{3,7},{5,1},{7,3},{8,12},{10,14},{12... | collective-permute-start | bytes 393224 | tf_op jit(solution)/shard_map/ppermute | solution.py:200
  30.8 14.7 %collective-permute-start.2 = (bf16[128,512]{1,0:T(8,128)(2,1)S(1)}, bf16[128,512]{1,0:T(8,128)(2,1)}, u32[]{:S(2)}, u32[]{:S(2)}) collective-permute-start(bf16[128,512]{1,0:T(8,128)(2,1)S(1)} %copy-done.2), channel_id=1, source_target_pairs={{0,6},{2,0},{4,2},{6,4},{1,7},{3,1},{5,3},{7,5},{8,14},{10,8},{12,... | collective-permute-start | bytes 393224 | tf_op jit(solution)/shard_map/ppermute | solution.py:200
  48.5 4.3 %collective-permute-start.4 = (bf16[4,4,32,512]{3,2,1,0:T(8,128)(2,1)S(1)}, bf16[4,4,32,512]{3,2,1,0:T(8,128)(2,1)S(1)}, u32[]{:S(2)}, u32[]{:S(2)}) collective-permute-start(bf16[4,4,32,512]{3,2,1,0:T(8,128)(2,1)S(1)} %shard_map.61), channel_id=1, source_target_pairs={{0,1},{1,0},{2,3},{3,2},{4,5},{5,4},{6,7},{7,6},{8,9},{9,8},{10,11... | collective-permute-start | bytes 1572872 | tf_op jit(solution)/shard_map/ppermute | solution.py:237
  50.4 10.6 %collective-permute-start.3 = (bf16[4,128,512]{2,1,0:T(8,128)(2,1)}, bf16[4,128,512]{2,1,0:T(8,128)(2,1)}, u32[]{:S(2)}, u32[]{:S(2)}) collective-permute-start(bf16[4,128,512]{2,1,0:T(8,128)(2,1)} %shard_map.59.refs_0_), channel_id=1, source_target_pairs={{0,1},{1,0},{2,3},{3,2},{4,5},{5,4},{6,7},{7,6},{8,9},{9,8},{10,11... | collective-permute-start | bytes 1572872 | tf_op jit(solution)/shard_map/ppermute | solution.py:220
  54.7 22.8 %all-to-all-start.1 = ((bf16[4,4,32,512]{3,2,1,0:T(8,128)(2,1)}), bf16[4,4,32,512]{3,2,1,0:T(8,128)(2,1)S(1)}, u32[]{:S(2)}, u32[]{:S(2)}) async-start(bf16[4,4,32,512]{3,2,1,0:T(8,128)(2,1)} %shard_map.62), calls=%async_computation.1 | async-start | bytes 1048576 | tf_op jit(solution)/shard_map/all_to_all | solution.py:18
  62.3 1.2 copy-start.3
  64.9 53.4 %copy-start.1 = (bf16[1024,1024]{1,0:T(8,128)(2,1)}, bf16[1024,1024]{1,0:T(8,128)(2,1)S(1)}, u32[]{:S(2)}) copy-start(bf16[1024,1024]{1,0:T(8,128)(2,1)S(1)} %convolution_convert_fusion.refs_0_) | copy-start | bytes 6291460

commit v7 on v6

--- a/solution.py
+++ b/solution.py
@@ -14,8 +14,17 @@
 SMALL = pltpu.CompilerParams(vmem_limit_bytes=12 * 2**20)
 
 
-def exchange(value, axes):
-    return lax.all_to_all(value, axes, split_axis=0, concat_axis=0, tiled=True)
+def exchange(value, axes, groups=None):
+    return lax.all_to_all(value, axes, split_axis=0, concat_axis=0, axis_index_groups=groups, tiled=True)
+
+
+def exchange_near(value):
+    groups = [
+        [(((yh + (core and yl == 0)) % NYH * NYL + yl) * NX + x) * NC + core for yl in range(NYL) for x in range(NX)]
+        for core in range(NC)
+        for yh in range(NYH)
+    ]
+    return exchange(value, ("yh", "yl", "x", "c"), groups)
 
 
 def lay_out(acts, cotangent):
@@ -174,7 +183,7 @@
     def kernel(value_ref, out_ref):
         for y in range(NYH):
             for zl, slot, row, column in where:
-                piece = value_ref[y, zl, slot : slot + PIECE]
+                piece = value_ref[zl, y, slot : slot + PIECE]
                 for s in range(NEAR):
                     out_ref[s, y, row : row + PIECE, column : column + LANES] = piece
 
@@ -231,7 +240,7 @@
     factor = (tok * NYH * NYL * NX * NZL * NZH * NC) ** (-0.5)
 
     core = lax.axis_index("c")[None]
-    got = exchange(lay_out(acts, cotangent), ("yl", "x")).reshape(NEAR * tok, NODE * part + head)
+    got = exchange_near(lay_out(acts, cotangent)).reshape(NEAR * tok, NODE * part + head)
     ordered = in_order(gather_zh(cotangent))
     theirs = product(got, head, 1 - core, after=[ordered])
     chip = product(got, head, core, received=lax.ppermute(theirs, "c", [(0, 1), (1, 0)]))
@@ -243,9 +252,9 @@
     slots = sum_y(over_y, [input_grad])
     slots = slots.reshape((NZH * NZL,) + slots.shape[2:])
     copies = sum_z(exchange(slots, ("zh", "zl")))
-    back = exchange(copies, ("yh", "zl"))
-    back = join(back.reshape((NYH, NZL) + back.shape[1:]), rows, head)
-    full = exchange(back, ("yl", "x")).reshape(owned, head)
+    back = exchange(copies, ("zl", "yh"))
+    back = join(back.reshape((NZL, NYH) + back.shape[1:]), rows, head)
+    full = exchange_near(back).reshape(owned, head)
     return (input_grad, full.astype(jnp.float32) * factor)
 
 

time: 137 us -> 136 us (level)
  no operation moved by 1% of the time
where the time goes in v7:
time: 136 us; the launch traced here: 135 us
  blocking collectives  55.8 us (41%)
  starting transfers between devices  39.7 us (29%)
  waiting for transfers between devices  24.9 us (18%)
  Pallas kernels  8.35 us (6%)
  other arithmetic  2.99 us (2%)
  matrix products  1.38 us (1%)
    all_to_all x3, blocking collectives, exchange(): lax.all_to_all(value, axes, split_axis=0, concat_axis=0, axis_index_group...  55.8 us
    all_to_all x2, starting transfers between devices, exchange(): lax.all_to_all(value, axes, split_axis=0, concat_axis=0, axis_index_group...  19.3 us
    ppermute x3, starting transfers between devices, gather_zh(): lax.ppermute(cotangent, 'zh', [(i, (i + k) % NZH) for i in range(NZH)])  16.1 us
    all_to_all x2, waiting for transfers between devices, exchange(): lax.all_to_all(value, axes, split_axis=0, concat_axis=0, axis_index_group...  12.5 us
    ppermute x3, waiting for transfers between devices, gather_zh(): lax.ppermute(cotangent, 'zh', [(i, (i + k) % NZH) for i in range(NZH)])  12.4 us
    pallas_call x1, Pallas kernels, lay_out(): pl.pallas_call(kernel, in_specs=[pl.BlockSpec(memory_space=pl.ANY)] * 2,...  3.3 us
    pallas_call x2, Pallas kernels, product(): pl.pallas_call(kernel, grid_spec=pltpu.PrefetchScalarGridSpec(num_scalar_...  3.06 us
  transfers between devices with their start and end apart: 7, of which 2 were waited for; matrix products, arithmetic and copies ran while one was open for 2% of the time, Pallas kernels for 3%

profile of v7, /device:TPU:8, one launch (start us, length us, event | category | flops | bytes accessed | tf_op | source)
XLA Modules:
  0.0 135.2 jit_solution(14726847658071264830)
XLA Ops:
  0.6 0.0 copy-start
  0.6 3.3 %shard_map.60 = bf16[8,128,1536]{2,1,0:T(8,128)(2,1)} custom-call(bf16[128,8192]{1,0:T(8,128)(2,1)} %acts_ref.1, bf16[128,512]{1,0:T(8,128)(2,1)} %cot_ref.1), custom_call_target="tpu_custom_call" | custom-call | bytes 6291456 | tf_op jit(solution)/shard_map/pallas_call | solution.py:64
  3.9 0.0 copy-start.2
  4.0 13.2 %all-to-all-start = ((bf16[8,128,1536]{2,1,0:T(8,128)(2,1)}), bf16[8,128,1536]{2,1,0:T(8,128)(2,1)S(1)}, u32[]{:S(2)}, u32[]{:S(2)}) async-start(bf16[8,128,1536]{2,1,0:T(8,128)(2,1)} %shard_map.60), calls=%async_computation | async-start | bytes 6291456 | tf_op jit(solution)/shard_map/all_to_all | solution.py:18
  17.1 1.9 %collective-permute-start = (bf16[128,512]{1,0:T(8,128)(2,1)S(1)}, bf16[128,512]{1,0:T(8,128)(2,1)S(1)}, u32[]{:S(2)}, u32[]{:S(2)}) collective-permute-start(bf16[128,512]{1,0:T(8,128)(2,1)S(1)} %copy-done.2), channel_id=1, source_target_pairs={{0,2},{2,4},{4,6},{6,0},{1,3},{3,5},{5,7},{7,1},{8,10},{10,12},{12... | collective-permute-start | bytes 393224 | tf_op jit(solution)/shard_map/ppermute | solution.py:209
  19.1 11.8 %collective-permute-start.1 = (bf16[128,512]{1,0:T(8,128)(2,1)S(1)}, bf16[128,512]{1,0:T(8,128)(2,1)S(1)}, u32[]{:S(2)}, u32[]{:S(2)}) collective-permute-start(bf16[128,512]{1,0:T(8,128)(2,1)S(1)} %copy-done.2), channel_id=1, source_target_pairs={{0,4},{2,6},{4,0},{6,2},{1,5},{3,7},{5,1},{7,3},{8,12},{10,14},{12... | collective-permute-start | bytes 393224 | tf_op jit(solution)/shard_map/ppermute | solution.py:209
  30.8 2.4 %collective-permute-start.2 = (bf16[128,512]{1,0:T(8,128)(2,1)S(1)}, bf16[128,512]{1,0:T(8,128)(2,1)}, u32[]{:S(2)}, u32[]{:S(2)}) collective-permute-start(bf16[128,512]{1,0:T(8,128)(2,1)S(1)} %copy-done.2), channel_id=1, source_target_pairs={{0,6},{2,0},{4,2},{6,4},{1,7},{3,1},{5,3},{7,5},{8,14},{10,8},{12,... | collective-permute-start | bytes 393224 | tf_op jit(solution)/shard_map/ppermute | solution.py:209
  33.3 12.4 %collective-permute-done.1.refs_2_ = bf16[128,512]{1,0:T(8,128)(2,1)S(1)} collective-permute-done((bf16[128,512]{1,0:T(8,128)(2,1)S(1)}, bf16[128,512]{1,0:T(8,128)(2,1)S(1)}, u32[]{:S(2)}, u32[]{:S(2)}) %collective-permute-start.1) | collective-permute-done | bytes 131104 | tf_op jit(solution)/shard_map/ppermute | solution.py:209
  45.7 0.0 collective-permute-done.2.refs_3_
  45.7 1.7 %shard_map.59.refs_0_ = bf16[4,128,512]{2,1,0:T(8,128)(2,1)} custom-call(s32[1]{0:T(128)} %bitcast.zh_ref, bf16[128,512]{1,0:T(8,128)(2,1)S(1)} %copy-done.2, bf16[128,512]{1,0:T(8,128)(2,1)S(1)} %collective-permute-done.refs_1_, bf16[128,512]{1,0:T(8,128)(2,1)S(1)} %collective-permute-done.1.refs_2_, bf16[128,512]{1,0:T(8,128)(2,1)} %collective-permute-done.2.refs_3_), custom_call_target="tpu_custom_call" | custom-call | bytes 1048576 | tf_op jit(solution)/shard_map/pallas_call | solution.py:218
  47.4 0.0 all-to-all-done
  47.4 1.2 shard_map.61
  48.6 1.9 %collective-permute-start.4 = (bf16[4,4,32,512]{3,2,1,0:T(8,128)(2,1)S(1)}, bf16[4,4,32,512]{3,2,1,0:T(8,128)(2,1)S(1)}, u32[]{:S(2)}, u32[]{:S(2)}) collective-permute-start(bf16[4,4,32,512]{3,2,1,0:T(8,128)(2,1)S(1)} %shard_map.61), channel_id=1, source_target_pairs={{0,1},{1,0},{2,3},{3,2},{4,5},{5,4},{6,7},{7,6},{8,9},{9,8},{10,11... | collective-permute-start | bytes 1572872 | tf_op jit(solution)/shard_map/ppermute | solution.py:246
  50.5 2.4 %collective-permute-start.3 = (bf16[4,128,512]{2,1,0:T(8,128)(2,1)}, bf16[4,128,512]{2,1,0:T(8,128)(2,1)}, u32[]{:S(2)}, u32[]{:S(2)}) collective-permute-start(bf16[4,128,512]{2,1,0:T(8,128)(2,1)} %shard_map.59.refs_0_), channel_id=1, source_target_pairs={{0,1},{1,0},{2,3},{3,2},{4,5},{5,4},{6,7},{7,6},{8,9},{9,8},{10,11... | collective-permute-start | bytes 1572872 | tf_op jit(solution)/shard_map/ppermute | solution.py:229
  52.9 0.0 collective-permute-done.4.refs_0_
  52.9 1.9 %shard_map.62 = bf16[4,4,32,512]{3,2,1,0:T(8,128)(2,1)} custom-call(s32[1]{0:T(128)} %bitcast.5.core_ref, bf16[1024,1536]{1,0:T(8,128)(2,1)S(1)} %bitcast.16, bf16[1024,1536]{1,0:T(8,128)(2,1)S(1)} %bitcast.17, bf16[4,4,32,512]{3,2,1,0:T(8,128)(2,1)S(1)} %collective-permute-done.4.refs_0_), custom_call_target="tpu_custom_call" | custom-call | flops 536870912 | bytes 3145728 | tf_op jit(solution)/shard_map/pallas_call | solution.py:103
  54.8 6.1 %all-to-all-start.1 = ((bf16[4,4,32,512]{3,2,1,0:T(8,128)(2,1)}), bf16[4,4,32,512]{3,2,1,0:T(8,128)(2,1)S(1)}, u32[]{:S(2)}, u32[]{:S(2)}) async-start(bf16[4,4,32,512]{3,2,1,0:T(8,128)(2,1)} %shard_map.62), calls=%async_computation.1 | async-start | bytes 1048576 | tf_op jit(solution)/shard_map/all_to_all | solution.py:18
  60.9 0.1 broadcast_bitcast_fusion
  61.0 1.3 select_bitcast_fusion.1
  62.3 0.0 copy-start.3
  62.3 0.1 pad_maximum_fusion
  62.4 0.1 copy.6
  62.5 1.0 copy-done.3
  63.5 1.4 %convolution_convert_fusion.refs_0_ = bf16[1024,1024]{1,0:T(8,128)(2,1)S(1)} fusion(bf16[1024,512]{1,0:T(8,128)(2,1)S(1)} %bitcast.21, bf16[1024,512]{1,0:T(8,128)(2,1)S(1)} %copy-done.3, f32[1024]{0:T(1024)S(1)} %broadcast_bitcast_fusion), kind=kOutput, calls=%fused_computation.2 | convolution fusion | flops 1076363264 | bytes 4198400 | tf_op jit(solution)/shard_map/dot_general | solution.py:201
  64.9 0.0 copy-start.1
  64.9 12.5 %all-to-all-done.1.value_ref = bf16[4,4,32,512]{3,2,1,0:T(8,128)(2,1)S(1)} async-done(((bf16[4,4,32,512]{3,2,1,0:T(8,128)(2,1)}), bf16[4,4,32,512]{3,2,1,0:T(8,128)(2,1)S(1)}, u32[]{:S(2)}, u32[]{:S(2)}) %all-to-all-start.1) | async-done | bytes 524320 | tf_op jit(solution)/shard_map/all_to_all | solution.py:18
  77.4 0.1 shard_map.63
  77.5 26.4 %all_to_all.25.value_ref = bf16[12,48,128]{2,1,0:T(8,128)(2,1)S(1)} all-to-all(bf16[12,48,128]{2,1,0:T(8,128)(2,1)S(1)} %bitcast.19), channel_id=1, replica_groups=mesh['yh'=4,'yl'=2,'x'=4,'zl'=3,'zh'=4,'c'=2] {'zh','zl'}, dimensions={0} | all-to-all | bytes 294912 | tf_op jit(solution)/shard_map/all_to_all | solution.py:18
  103.9 13.8 %all_to_all.26 = bf16[12,48,128]{2,1,0:T(8,128)(2,1)S(1)} all-to-all(bf16[12,48,128]{2,1,0:T(8,128)(2,1)S(1)} %shard_map.64), channel_id=1, replica_groups=mesh['yh'=4,'yl'=2,'x'=4,'zl'=3,'zh'=4,'c'=2] {'zl','yh'}, dimensions={0} | all-to-all | bytes 294912 | tf_op jit(solution)/shard_map/all_to_all | solution.py:18
  117.6 0.2 shard_map.65
  117.8 15.7 %all_to_all.27 = bf16[8,4,32,512]{3,2,1,0:T(8,128)(2,1)S(1)} all-to-all(bf16[8,4,32,512]{3,2,1,0:T(8,128)(2,1)S(1)} %shard_map.65), channel_id=1, replica_groups={{0,24,48,72,96,120,144,168},{192,216,240,264,288,312,336,360},{384,408,..., dimensions={0} | all-to-all | bytes 2097152 | tf_op jit(solution)/shard_map/all_to_all | solution.py:18
  133.5 1.6 %convert_multiply_fusion = f32[8,4,32,512]{3,2,1,0:T(8,128)} fusion(bf16[8,4,32,512]{3,2,1,0:T(8,128)(2,1)S(1)} %all_to_all.27), kind=kLoop, calls=%fused_computation | loop fusion | flops 1048576 | bytes 3145728 | tf_op jit(solution)/shard_map/mul | solution.py:258
  (6 shorter events, 0.0 us)
Async XLA Ops:
  0.6 60.3 %copy-start = (f32[8]{0:T(128)S(1)}, f32[8]{0:T(128)}, u32[]{:S(2)}) copy-start(f32[8]{0:T(128)} %param.7) | copy-start | bytes 100
  3.9 13.2 %copy-start.2 = (bf16[128,512]{1,0:T(8,128)(2,1)S(1)}, bf16[128,512]{1,0:T(8,128)(2,1)}, u32[]{:S(2)}) copy-start(bf16[128,512]{1,0:T(8,128)(2,1)} %cot_ref.1) | copy-start | bytes 393220
  4.0 43.4 %all-to-all-start = ((bf16[8,128,1536]{2,1,0:T(8,128)(2,1)}), bf16[8,128,1536]{2,1,0:T(8,128)(2,1)S(1)}, u32[]{:S(2)}, u32[]{:S(2)}) async-start(bf16[8,128,1536]{2,1,0:T(8,128)(2,1)} %shard_map.60), calls=%async_computation | async-start | bytes 6291456 | tf_op jit(solution)/shard_map/all_to_all | solution.py:18
  17.1 16.1 %collective-permute-start = (bf16[128,512]{1,0:T(8,128)(2,1)S(1)}, bf16[128,512]{1,0:T(8,128)(2,1)S(1)}, u32[]{:S(2)}, u32[]{:S(2)}) collective-permute-start(bf16[128,512]{1,0:T(8,128)(2,1)S(1)} %copy-done.2), channel_id=1, source_target_pairs={{0,2},{2,4},{4,6},{6,0},{1,3},{3,5},{5,7},{7,1},{8,10},{10,12},{12... | collective-permute-start | bytes 393224 | tf_op jit(solution)/shard_map/ppermute | solution.py:209
  19.1 26.6 %collective-permute-start.1 = (bf16[128,512]{1,0:T(8,128)(2,1)S(1)}, bf16[128,512]{1,0:T(8,128)(2,1)S(1)}, u32[]{:S(2)}, u32[]{:S(2)}) collective-permute-start(bf16[128,512]{1,0:T(8,128)(2,1)S(1)} %copy-done.2), channel_id=1, source_target_pairs={{0,4},{2,6},{4,0},{6,2},{1,5},{3,7},{5,1},{7,3},{8,12},{10,14},{12... | collective-permute-start | bytes 393224 | tf_op jit(solution)/shard_map/ppermute | solution.py:209
  30.8 14.9 %collective-permute-start.2 = (bf16[128,512]{1,0:T(8,128)(2,1)S(1)}, bf16[128,512]{1,0:T(8,128)(2,1)}, u32[]{:S(2)}, u32[]{:S(2)}) collective-permute-start(bf16[128,512]{1,0:T(8,128)(2,1)S(1)} %copy-done.2), channel_id=1, source_target_pairs={{0,6},{2,0},{4,2},{6,4},{1,7},{3,1},{5,3},{7,5},{8,14},{10,8},{12,... | collective-permute-start | bytes 393224 | tf_op jit(solution)/shard_map/ppermute | solution.py:209
  48.6 4.3 %collective-permute-start.4 = (bf16[4,4,32,512]{3,2,1,0:T(8,128)(2,1)S(1)}, bf16[4,4,32,512]{3,2,1,0:T(8,128)(2,1)S(1)}, u32[]{:S(2)}, u32[]{:S(2)}) collective-permute-start(bf16[4,4,32,512]{3,2,1,0:T(8,128)(2,1)S(1)} %shard_map.61), channel_id=1, source_target_pairs={{0,1},{1,0},{2,3},{3,2},{4,5},{5,4},{6,7},{7,6},{8,9},{9,8},{10,11... | collective-permute-start | bytes 1572872 | tf_op jit(solution)/shard_map/ppermute | solution.py:246
  50.5 10.5 %collective-permute-start.3 = (bf16[4,128,512]{2,1,0:T(8,128)(2,1)}, bf16[4,128,512]{2,1,0:T(8,128)(2,1)}, u32[]{:S(2)}, u32[]{:S(2)}) collective-permute-start(bf16[4,128,512]{2,1,0:T(8,128)(2,1)} %shard_map.59.refs_0_), channel_id=1, source_target_pairs={{0,1},{1,0},{2,3},{3,2},{4,5},{5,4},{6,7},{7,6},{8,9},{9,8},{10,11... | collective-permute-start | bytes 1572872 | tf_op jit(solution)/shard_map/ppermute | solution.py:229
  54.8 22.6 %all-to-all-start.1 = ((bf16[4,4,32,512]{3,2,1,0:T(8,128)(2,1)}), bf16[4,4,32,512]{3,2,1,0:T(8,128)(2,1)S(1)}, u32[]{:S(2)}, u32[]{:S(2)}) async-start(bf16[4,4,32,512]{3,2,1,0:T(8,128)(2,1)} %shard_map.62), calls=%async_computation.1 | async-start | bytes 1048576 | tf_op jit(solution)/shard_map/all_to_all | solution.py:18
  62.3 1.2 copy-start.3
  64.9 52.9 %copy-start.1 = (bf16[1024,1024]{1,0:T(8,128)(2,1)}, bf16[1024,1024]{1,0:T(8,128)(2,1)S(1)}, u32[]{:S(2)}) copy-start(bf16[1024,1024]{1,0:T(8,128)(2,1)S(1)} %convolution_convert_fusion.refs_0_) | copy-start | bytes 6291460
